TPU v7x, 32 devices: a whole 2x2x4 slice. The times are simulated.
32 devices in a mesh: dp: 8 (over z, core), fsdp: 4 (over y, x).
Axes of the slice: x: 2, y: 2, z: 4, core: 2. Of those that a mesh axis runs over, the one named last changes fastest.
Arguments:
- layer_input: bfloat16 [32768, 1024], P(('dp', 'fsdp')), may hold values from -6 to 6
- segment_ids: int32 [32768], P(('dp', 'fsdp')), may hold values from 0 to 4, as said below
- relative_buckets: int32 [2047], replicated, may hold values from 0 to 31, as said below
- first_gain: bfloat16 [1024], P(('dp', 'fsdp')), may hold values from 0.5 to 1.5
- query_weight: bfloat16 [1024, 1024], P(('dp', 'fsdp')), may hold values from -0.0625 to 0.0625
- key_weight: bfloat16 [1024, 1024], P(('dp', 'fsdp')), may hold values from -0.0625 to 0.0625
- value_weight: bfloat16 [1024, 1024], P(('dp', 'fsdp')), may hold values from -0.1875 to 0.1875
- output_projection: bfloat16 [1024, 1024], P(('dp', 'fsdp')), may hold values from -0.75 to 0.75
- relative_table: bfloat16 [32, 16], replicated, may hold values from -5 to 5
- second_gain: bfloat16 [1024], P(('dp', 'fsdp')), may hold values from 0.5 to 1.5
- gate_weight: bfloat16 [1024, 2816], P(('dp', 'fsdp')), may hold values from -0.1875 to 0.1875
- up_weight: bfloat16 [1024, 2816], P(('dp', 'fsdp')), may hold values from -0.1875 to 0.1875
- down_projection: bfloat16 [1024, 2816], P(('dp', 'fsdp')), may hold values from -0.15625 to 0.15625
- output_cotangent: bfloat16 [32768, 1024], P(('dp', 'fsdp')), may hold values from -6 to 6
Outputs:
- block_output: bfloat16 [32768, 1024], P(('dp', 'fsdp'))
- input_gradient: float32 [32768, 1024], P(('dp', 'fsdp'))
- query_gradient: float32 [1024, 1024], P(('dp', 'fsdp'))
- key_gradient: float32 [1024, 1024], P(('dp', 'fsdp'))
- value_gradient: float32 [1024, 1024], P(('dp', 'fsdp'))
- output_gradient: float32 [1024, 1024], P(('dp', 'fsdp'))
- gate_gradient: float32 [1024, 2816], P(('dp', 'fsdp'))
- up_gradient: float32 [1024, 2816], P(('dp', 'fsdp'))
- down_gradient: float32 [1024, 2816], P(('dp', 'fsdp'))
- first_gain_gradient: float32 [1024], P(('dp', 'fsdp'))
- second_gain_gradient: float32 [1024], P(('dp', 'fsdp'))
- table_gradient: float32 [32, 16], replicated
Inputs may be any that keep to these rules, and one draw needn't show every extreme that they name: `segment_ids`: each packed row of 1024 tokens holds 4 image-text pairs numbered 1 to 4 in order, each a run of consecutive positions, then padding with id 0 to the row's end; a row holds 512 to 1024 live tokens, and some row has no padding. `relative_buckets`: entry 1023 + r is the bucket of the offset r = key position minus query position; it is 0 at r = 0, never falls as the size of r grows on either side, lies in 1 to 15 for r < 0 and in 16 to 31 for r > 0, and the largest offsets of both sides take the largest buckets of their side.
All inputs are finite; a program needn't handle non-finite values.
Results may differ from a plain program's by a relative error of at most 0.015.
Values may be sent and summed in bfloat16 or wider, within the bound.
No kernel may reach another device: no remote copies, remote signals or barrier semaphores. Data moves between devices by JAX's collectives and lax.ppermute only.
A program may use at most 192 MiB of HBM per device.

v0:
```python
import jax
import jax.numpy as jnp
from jax import lax
from jax.sharding import PartitionSpec as P

HEADS = 16
HEAD_DIM = 64
BUCKETS = 32
SEQ = 1024


EPS = 1e-06
NEGATIVE = -1e30
HIGHEST_ACCURACY = lax.Precision.HIGHEST


def norm_rows(values, gain):
    return values * lax.rsqrt(jnp.mean(values * values, axis=-1, keepdims=True) + EPS) * gain


def contract(left, right, left_dim, right_dim):
    return lax.dot_general(
        left, right, (((left_dim,), (right_dim,)), ((), ())), preferred_element_type=jnp.float32
    )


def diagonal_sums(matrix, length):
    flipped = matrix[:, ::-1]
    padded = jnp.concatenate([flipped, jnp.zeros((length, length), matrix.dtype)], axis=-1)
    flat = padded.reshape((2 * length * length,))[: length * (2 * length - 1)]
    return jnp.sum(flat.reshape((length, 2 * length - 1)), axis=0)[::-1]


def build_bias(offset_pair, length):
    count = offset_pair.shape[0]
    padded = jnp.concatenate([offset_pair, jnp.zeros((count, 1), offset_pair.dtype)], axis=-1)
    flat = jnp.tile(padded, (1, length))
    window = flat[:, length - 1 : length - 1 + length * (2 * length - 1)]
    return window.reshape(count, length, 2 * length - 1)[:, :, :length]


def pair_slice(matrix, pair_index, width):
    return lax.dynamic_slice_in_dim(matrix, pair_index * width, width, 2)


def on_device(
    layer_input,
    segment_ids,
    relative_buckets,
    first_gain,
    query_weight,
    key_weight,
    value_weight,
    output_projection,
    relative_table,
    second_gain,
    gate_weight,
    up_weight,
    down_projection,
    output_cotangent,
):
    length = SEQ
    width = 2 * HEAD_DIM
    seq_count = layer_input.shape[0] // length
    live = (segment_ids > 0).astype(jnp.float32)[:, None]
    segments = segment_ids.reshape(seq_count, length)
    allowed = (segments[:, :, None] == segments[:, None, :]) & (segments[:, None, :] > 0)
    one_hot = (relative_buckets[:, None] == jnp.arange(BUCKETS)[None, :]).astype(jnp.float32)
    offsets_rows = jnp.take(relative_table.T, relative_buckets, axis=1)
    lanes = jnp.arange(width)
    lane_masks = [(lanes // HEAD_DIM == half).astype(jnp.bfloat16) for half in range(2)]

    def pair_bias(pair_index):
        return build_bias(lax.dynamic_slice_in_dim(offsets_rows, pair_index * 2, 2, 0), length)

    def head_scores(query_head, key_pair, bias_head):
        scores = jnp.einsum(
            "sqd,skd->sqk", query_head, key_pair, preferred_element_type=jnp.float32
        )
        scores = scores + bias_head.astype(jnp.float32)[None]
        return jnp.where(allowed, scores, NEGATIVE)

    def forward_pair(pair_index, carry):
        attended_buf, lse_buf = carry
        query_pair = pair_slice(query3, pair_index, width)
        key_pair = pair_slice(keys3, pair_index, width)
        value_pair = pair_slice(values3, pair_index, width)
        bias_pair = pair_bias(pair_index)
        mixed_pair = jnp.zeros((seq_count, length, width), jnp.float32)
        for half in range(2):
            scores = head_scores(query_pair * lane_masks[half], key_pair, bias_pair[half])
            peak = jnp.max(scores, axis=-1, keepdims=True)
            raised = jnp.exp(scores - peak)
            total = jnp.sum(raised, axis=-1, keepdims=True)
            prob = (raised / total).astype(jnp.bfloat16)
            product = jnp.einsum(
                "sqk,skd->sqd", prob, value_pair, preferred_element_type=jnp.float32
            )
            mixed_pair = mixed_pair + product * lane_masks[half].astype(jnp.float32)
            lse_buf = lax.dynamic_update_index_in_dim(
                lse_buf, (peak + jnp.log(total))[..., 0], pair_index * 2 + half, 0
            )
        attended_buf = lax.dynamic_update_slice_in_dim(
            attended_buf, mixed_pair.astype(jnp.bfloat16), pair_index * width, 2
        )
        return (attended_buf, lse_buf)

    def backward_pair(pair_index, carry):
        query_buf, key_buf, value_buf, offset_buf = carry
        query_pair = pair_slice(query3, pair_index, width)
        key_pair = pair_slice(keys3, pair_index, width)
        value_pair = pair_slice(values3, pair_index, width)
        grad_pair = pair_slice(grad3, pair_index, width)
        bias_pair = pair_bias(pair_index)
        query_acc = jnp.zeros((seq_count, length, width), jnp.float32)
        key_acc = jnp.zeros((seq_count, length, width), jnp.float32)
        value_acc = jnp.zeros((seq_count, length, width), jnp.float32)
        for half in range(2):
            mask_low = lane_masks[half]
            mask_wide = mask_low.astype(jnp.float32)
            query_head = query_pair * mask_low
            grad_head = grad_pair * mask_low
            scores = head_scores(query_head, key_pair, bias_pair[half])
            log_total = lax.dynamic_index_in_dim(lse_buf, pair_index * 2 + half, 0, keepdims=False)
            prob = jnp.exp(scores - log_total[..., None])
            prob_grad = jnp.einsum(
                "sqd,skd->sqk", grad_head, value_pair, preferred_element_type=jnp.float32
            )
            inner = jnp.sum(prob * prob_grad, axis=-1, keepdims=True)
            scores_grad = (prob * (prob_grad - inner)).astype(jnp.bfloat16)
            value_acc = value_acc + jnp.einsum(
                "sqk,sqd->skd",
                prob.astype(jnp.bfloat16),
                grad_head,
                preferred_element_type=jnp.float32,
            )
            query_acc = (
                query_acc
                + jnp.einsum(
                    "sqk,skd->sqd", scores_grad, key_pair, preferred_element_type=jnp.float32
                )
                * mask_wide
            )
            key_acc = key_acc + jnp.einsum(
                "sqk,sqd->skd", scores_grad, query_head, preferred_element_type=jnp.float32
            )
            offset_grad = diagonal_sums(jnp.sum(scores_grad.astype(jnp.float32), axis=0), length)
            offset_buf = lax.dynamic_update_index_in_dim(
                offset_buf, offset_grad, pair_index * 2 + half, 0
            )
        query_buf = lax.dynamic_update_slice_in_dim(
            query_buf, query_acc.astype(jnp.bfloat16), pair_index * width, 2
        )
        key_buf = lax.dynamic_update_slice_in_dim(
            key_buf, key_acc.astype(jnp.bfloat16), pair_index * width, 2
        )
        value_buf = lax.dynamic_update_slice_in_dim(
            value_buf, value_acc.astype(jnp.bfloat16), pair_index * width, 2
        )
        return (query_buf, key_buf, value_buf, offset_buf)

    input_rows = layer_input.astype(jnp.float32)
    attention_set = (
        lax.all_gather(first_gain, ("dp", "fsdp"), axis=0, tiled=True),
        lax.all_gather(query_weight, ("dp", "fsdp"), axis=0, tiled=True),
        lax.all_gather(key_weight, ("dp", "fsdp"), axis=0, tiled=True),
        lax.all_gather(value_weight, ("dp", "fsdp"), axis=0, tiled=True),
        lax.all_gather(output_projection, ("dp", "fsdp"), axis=0, tiled=True),
    )
    gain_one, query_full, key_full, value_full, output_full = attention_set
    normed = norm_rows(input_rows, gain_one.astype(jnp.float32)).astype(jnp.bfloat16)
    query = jnp.dot(normed, query_full, preferred_element_type=jnp.float32).astype(jnp.bfloat16)
    keys = jnp.dot(normed, key_full, preferred_element_type=jnp.float32).astype(jnp.bfloat16)
    values = jnp.dot(normed, value_full, preferred_element_type=jnp.float32).astype(jnp.bfloat16)
    inner_width = query.shape[1]
    query3 = query.reshape(seq_count, length, inner_width)
    keys3 = keys.reshape(seq_count, length, inner_width)
    values3 = values.reshape(seq_count, length, inner_width)
    start_attended = jnp.zeros((seq_count, length, inner_width), jnp.bfloat16)
    start_lse = jnp.zeros((HEADS, seq_count, length), jnp.float32)
    attended3, lse_buf = lax.fori_loop(0, HEADS // 2, forward_pair, (start_attended, start_lse))
    attended_values = attended3.reshape(seq_count * length, inner_width)
    hidden_units = input_rows + contract(attended_values, output_full, 1, 1)
    feed_set = (
        lax.all_gather(second_gain, ("dp", "fsdp"), axis=0, tiled=True),
        lax.all_gather(gate_weight, ("dp", "fsdp"), axis=0, tiled=True),
        lax.all_gather(up_weight, ("dp", "fsdp"), axis=0, tiled=True),
        lax.all_gather(down_projection, ("dp", "fsdp"), axis=0, tiled=True),
    )
    gain_two, gate_full, up_full, down_full = feed_set
    normed_two = norm_rows(hidden_units, gain_two.astype(jnp.float32)).astype(jnp.bfloat16)
    gate = jnp.dot(normed_two, gate_full, preferred_element_type=jnp.float32)
    upward = jnp.dot(normed_two, up_full, preferred_element_type=jnp.float32)
    mixed_units = (jax.nn.gelu(gate, approximate=True) * upward).astype(jnp.bfloat16)
    block_output = ((hidden_units + contract(mixed_units, down_full, 1, 1)) * live).astype(
        jnp.bfloat16
    )
    cotangent = output_cotangent.astype(jnp.float32) * live
    gain_two, gate_full, up_full, down_full = (
        lax.all_gather(second_gain, ("dp", "fsdp"), axis=0, tiled=True),
        lax.all_gather(gate_weight, ("dp", "fsdp"), axis=0, tiled=True),
        lax.all_gather(up_weight, ("dp", "fsdp"), axis=0, tiled=True),
        lax.all_gather(down_projection, ("dp", "fsdp"), axis=0, tiled=True),
    )
    cotangent_low = cotangent.astype(jnp.bfloat16)
    mixed_grad = jnp.dot(cotangent_low, down_full, preferred_element_type=jnp.float32)
    down_term = contract(cotangent_low, mixed_units, 0, 0)

    def gated(gate_in, upward_in):
        return jax.nn.gelu(gate_in, approximate=True) * upward_in

    unused_value, gated_pull = jax.vjp(gated, gate, upward)
    gate_grad, upward_grad = gated_pull(mixed_grad)
    gate_grad = gate_grad.astype(jnp.bfloat16)
    upward_grad = upward_grad.astype(jnp.bfloat16)
    gate_term = contract(normed_two, gate_grad, 0, 0)
    up_term = contract(normed_two, upward_grad, 0, 0)
    normed_two_grad = contract(gate_grad, gate_full, 1, 1) + contract(upward_grad, up_full, 1, 1)
    unused_two, norm_two_pull = jax.vjp(norm_rows, hidden_units, gain_two.astype(jnp.float32))
    hidden_part, second_gain_term = norm_two_pull(normed_two_grad)
    hidden_grad = cotangent + hidden_part
    gain_one, query_full, key_full, value_full, output_full = (
        lax.all_gather(first_gain, ("dp", "fsdp"), axis=0, tiled=True),
        lax.all_gather(query_weight, ("dp", "fsdp"), axis=0, tiled=True),
        lax.all_gather(key_weight, ("dp", "fsdp"), axis=0, tiled=True),
        lax.all_gather(value_weight, ("dp", "fsdp"), axis=0, tiled=True),
        lax.all_gather(output_projection, ("dp", "fsdp"), axis=0, tiled=True),
    )
    branch_grad = hidden_grad.astype(jnp.bfloat16)
    output_term = contract(branch_grad, attended_values, 0, 0)
    attended_grad = jnp.dot(branch_grad, output_full, preferred_element_type=jnp.float32).astype(
        jnp.bfloat16
    )
    grad3 = attended_grad.reshape(seq_count, length, inner_width)
    start_grads = (
        jnp.zeros((seq_count, length, inner_width), jnp.bfloat16),
        jnp.zeros((seq_count, length, inner_width), jnp.bfloat16),
        jnp.zeros((seq_count, length, inner_width), jnp.bfloat16),
        jnp.zeros((HEADS, 2 * length - 1), jnp.float32),
    )
    query_buf, key_buf, value_buf, offset_grads = lax.fori_loop(
        0, HEADS // 2, backward_pair, start_grads
    )
    query_grad = query_buf.reshape(seq_count * length, inner_width)
    keys_grad = key_buf.reshape(seq_count * length, inner_width)
    values_grad = value_buf.reshape(seq_count * length, inner_width)
    query_term = contract(normed, query_grad, 0, 0)
    key_term = contract(normed, keys_grad, 0, 0)
    value_term = contract(normed, values_grad, 0, 0)
    normed_grad = (
        contract(query_grad, query_full, 1, 1)
        + contract(keys_grad, key_full, 1, 1)
        + contract(values_grad, value_full, 1, 1)
    )
    unused_one, norm_one_pull = jax.vjp(norm_rows, input_rows, gain_one.astype(jnp.float32))
    input_part, first_gain_term = norm_one_pull(normed_grad)
    input_gradient = hidden_grad + input_part
    table_term = jnp.dot(one_hot.T, offset_grads.T, precision=HIGHEST_ACCURACY)
    table_gradient = lax.psum(table_term, ("dp", "fsdp"))
    all_sums = (
        lax.psum_scatter(query_term, ("dp", "fsdp"), scatter_dimension=0, tiled=True),
        lax.psum_scatter(key_term, ("dp", "fsdp"), scatter_dimension=0, tiled=True),
        lax.psum_scatter(value_term, ("dp", "fsdp"), scatter_dimension=0, tiled=True),
        lax.psum_scatter(output_term, ("dp", "fsdp"), scatter_dimension=0, tiled=True),
        lax.psum_scatter(first_gain_term, ("dp", "fsdp"), scatter_dimension=0, tiled=True),
        lax.psum_scatter(gate_term, ("dp", "fsdp"), scatter_dimension=0, tiled=True),
        lax.psum_scatter(up_term, ("dp", "fsdp"), scatter_dimension=0, tiled=True),
        lax.psum_scatter(down_term, ("dp", "fsdp"), scatter_dimension=0, tiled=True),
        lax.psum_scatter(second_gain_term, ("dp", "fsdp"), scatter_dimension=0, tiled=True),
    )
    attention_sums = all_sums[:5]
    feed_sums = all_sums[5:]
    return (
        block_output,
        input_gradient,
        attention_sums[0],
        attention_sums[1],
        attention_sums[2],
        attention_sums[3],
        feed_sums[0],
        feed_sums[1],
        feed_sums[2],
        attention_sums[4],
        feed_sums[3],
        table_gradient,
    )


def solution(mesh):
    return jax.shard_map(
        on_device,
        mesh=mesh,
        in_specs=(
            P(("dp", "fsdp"), None),
            P(("dp", "fsdp")),
            P(),
            P(("dp", "fsdp")),
            P(("dp", "fsdp"), None),
            P(("dp", "fsdp"), None),
            P(("dp", "fsdp"), None),
            P(("dp", "fsdp"), None),
            P(),
            P(("dp", "fsdp")),
            P(("dp", "fsdp"), None),
            P(("dp", "fsdp"), None),
            P(("dp", "fsdp"), None),
            P(("dp", "fsdp"), None),
        ),
        out_specs=(
            P(("dp", "fsdp"), None),
            P(("dp", "fsdp"), None),
            P(("dp", "fsdp"), None),
            P(("dp", "fsdp"), None),
            P(("dp", "fsdp"), None),
            P(("dp", "fsdp"), None),
            P(("dp", "fsdp"), None),
            P(("dp", "fsdp"), None),
            P(("dp", "fsdp"), None),
            P(("dp", "fsdp")),
            P(("dp", "fsdp")),
            P(),
        ),
        check_vma=False,
    )
```

profile of v0, /device:TPU:0, one launch (start us, length us, event | category | flops | bytes accessed | tf_op | source)
XLA Modules:
  0.0 4013.4 jit_solution(1983445005110652261)
XLA Ops:
  16.8 42.4 %all-reduce.9 = (bf16[1024]{0:T(1024)(128)(2,1)S(1)}, bf16[1024]{0:T(1024)(128)(2,1)S(1)}) all-reduce(bf16[1024]{0:T(1024)(128)(2,1)S(1)} %dynamic-update-slice, bf16[1024]{0:T(1024)(128)(2,1)S(1)} %dynamic-update-slice.1), channel_id=1, replica_groups=mesh['dp'=8,'fsdp'=4] {'dp','fsdp'}, use_global_device_ids=true, to_apply=%add.4 | all-reduce | flops 2048 | bytes 8192
  77.6 50.8 %all-gather.10.cloned.1.call-done = bf16[1024,1024]{1,0:T(8,128)(2,1)} async-done(((bf16[32,1024]{1,0:T(8,128)(2,1)}), bf16[1024,1024]{1,0:T(8,128)(2,1)}) %all-gather.10.cloned.1.call-update) | async-done | bytes 2097168 | tf_op jit(solution)/shard_map/all_gather | solution.py:166
  134.0 52.6 %all-gather.12.cloned.1.call-done = bf16[1024,1024]{1,0:T(8,128)(2,1)} async-done(((bf16[32,1024]{1,0:T(8,128)(2,1)}), bf16[1024,1024]{1,0:T(8,128)(2,1)}) %all-gather.12.cloned.1.call-update) | async-done | bytes 2097168 | tf_op jit(solution)/shard_map/all_gather | solution.py:167
  193.7 651.0 %while.42 = (s32[]{:T(128)}, bf16[1,1024,1024]{2,1,0:T(8,128)(2,1)}, f32[16,1,1024]{2,1,0:T(1,128)S(1)}, bf16[1,1024,1024]{2,1,0:T(8,128)(2,1)}, bf16[1,1024,102...) while((s32[]{:T(128)}, ...), condition=%wide.region_6.7_spmd.clone.clone, body=%wide.region_1.0_spmd.clone.clone.sunk | while | flops 1098384640 | bytes 124642096 | solution.py:181
  877.4 22.5 multiply_convert_fusion.2
  928.2 1749.6 %while.43 = (s32[]{:T(128)}, bf16[1,1024,1024]{2,1,0:T(8,128)(2,1)}, bf16[1,1024,1024]{2,1,0:T(8,128)(2,1)}, bf16[1,1024,1024]{2,1,0:T(8,128)(2,1)}, f32[16,2047...) while((s32[]{:T(128)}, ...), condition=%wide.region_14.15_spmd.clone.clone, body=%wide.region_9.14_spmd.clone.clone.sunk | while | flops 2718952704 | bytes 439786368 | solution.py:241
  1032.0 31.0 rev.40
  1249.5 31.0 rev.40
  1467.2 31.0 rev.40
  1528.9 21.6 rev.41
  1684.7 31.0 rev.40
  1902.4 31.0 rev.40
  1964.1 21.6 rev.41
  2119.9 31.0 rev.40
  2337.7 31.0 rev.40
  2399.4 21.6 rev.41
  2555.2 31.0 rev.40
  2776.9 39.4 all-reduce.8
  2825.0 142.5 %reduce-scatter.10.cloned.1.call-done = f32[32,1024]{1,0:T(8,128)} async-done(((f32[1024,1024]{1,0:T(8,128)}), f32[32,1024]{1,0:T(8,128)}) %reduce-scatter.10.cloned.1.call-update) | async-done | bytes 131088 | tf_op jit(solution)/shard_map/reduce_scatter | solution.py:262
  2967.5 142.3 %reduce-scatter.12.cloned.1.call-done = f32[32,1024]{1,0:T(8,128)} async-done(((f32[1024,1024]{1,0:T(8,128)}), f32[32,1024]{1,0:T(8,128)}) %reduce-scatter.12.cloned.1.call-update) | async-done | bytes 131088 | tf_op jit(solution)/shard_map/reduce_scatter | solution.py:263
  3109.8 141.5 %reduce-scatter.14.cloned.1.call-done = f32[32,1024]{1,0:T(8,128)} async-done(((f32[1024,1024]{1,0:T(8,128)}), f32[32,1024]{1,0:T(8,128)}) %reduce-scatter.14.cloned.1.call-update) | async-done | bytes 131088 | tf_op jit(solution)/shard_map/reduce_scatter | solution.py:264
  3251.3 249.8 %reduce-scatter.16.cloned.1.call-done = f32[32,2816]{1,0:T(8,128)} async-done(((f32[1024,2816]{1,0:T(8,128)}), f32[32,2816]{1,0:T(8,128)}) %reduce-scatter.16.cloned.1.call-update) | async-done | bytes 360464 | tf_op jit(solution)/shard_map/reduce_scatter | solution.py:266
  3501.1 252.7 %reduce-scatter.18.cloned.1.call-done = f32[32,2816]{1,0:T(8,128)} async-done(((f32[1024,2816]{1,0:T(8,128)}), f32[32,2816]{1,0:T(8,128)}) %reduce-scatter.18.cloned.1.call-update) | async-done | bytes 360464 | tf_op jit(solution)/shard_map/reduce_scatter | solution.py:267
  3753.8 252.7 %reduce-scatter.20.cloned.1.call-done = f32[32,2816]{1,0:T(8,128)} async-done(((f32[1024,2816]{1,0:T(8,128)}), f32[32,2816]{1,0:T(8,128)}) %reduce-scatter.20.cloned.1.call-update) | async-done | bytes 360464 | tf_op jit(solution)/shard_map/reduce_scatter | solution.py:268
  (832 shorter events, 2282.6 us)
Async XLA Ops:
  7.2 53.0 %copy-start.32 = (bf16[32,16]{0,1:T(8,128)(2,1)S(1)}, bf16[32,16]{0,1:T(8,128)(2,1)}, u32[]{:S(2)}) copy-start(bf16[32,16]{0,1:T(8,128)(2,1)} %param.26) | copy-start | bytes 3076
  7.2 65.0 %all-gather.8.cloned.1.call-start = ((), (), s32[]{:S(2)}) async-start(), calls=%async_computation.7 | async-start | bytes 2162688 | tf_op jit(solution)/shard_map/all_gather | solution.py:165
  7.9 120.5 %all-gather.10.cloned.1.call-start = ((), (), s32[]{:S(2)}) async-start(), calls=%async_computation.8 | async-start | bytes 2162688 | tf_op jit(solution)/shard_map/all_gather | solution.py:166
  8.7 177.9 %all-gather.12.cloned.1.call-start = ((), (), s32[]{:S(2)}) async-start(), calls=%async_computation.9 | async-start | bytes 2162688 | tf_op jit(solution)/shard_map/all_gather | solution.py:167
  9.4 835.3 %all-gather.14.cloned.1.call-start = ((), (), s32[]{:S(2)}) async-start(), calls=%async_computation.10 | async-start | bytes 2162688 | tf_op jit(solution)/shard_map/all_gather | solution.py:168
  10.0 842.5 %all-gather.16.cloned.1.call-start = ((), (), s32[]{:S(2)}) async-start(), calls=%async_computation.11 | async-start | bytes 5947392 | tf_op jit(solution)/shard_map/all_gather | solution.py:186
  10.6 854.8 %all-gather.18.cloned.1.call-start = ((), (), s32[]{:S(2)}) async-start(), calls=%async_computation.12 | async-start | bytes 5947392 | tf_op jit(solution)/shard_map/all_gather | solution.py:187
  11.2 866.2 %all-gather.20.cloned.1.call-start = ((), (), s32[]{:S(2)}) async-start(), calls=%async_computation.13 | async-start | bytes 5947392 | tf_op jit(solution)/shard_map/all_gather | solution.py:188
  11.9 2813.1 %reduce-scatter.8.cloned.1.call-start = ((), (), s32[]{:S(2)}) async-start(), calls=%async_computation.14 | async-start | bytes 4325376 | tf_op jit(solution)/shard_map/reduce_scatter | solution.py:261
  13.4 53.6 %copy-start.19 = (s32[1024]{0:T(1024)S(1)}, s32[1024]{0:T(1024)}, u32[]{:S(2)}) copy-start(s32[1024]{0:T(1024)} %param.19) | copy-start | bytes 12292
  16.2 170.4 %copy-start.6 = (bf16[1024,1024]{0,1:T(8,128)(2,1)}, bf16[1024,1024]{0,1:T(8,128)(2,1)S(1)}, u32[]{:S(2)}) copy-start(bf16[1024,1024]{0,1:T(8,128)(2,1)S(1)} %copy.83) | copy-start | bytes 6291460
  59.1 127.5 %copy-start.24 = (f32[1024]{0:T(1024)}, f32[1024]{0:T(1024)S(1)}, u32[]{:S(2)}) copy-start(f32[1024]{0:T(1024)S(1)} %convert_element_type.325) | copy-start | bytes 12292
  60.2 126.4 %copy-start.20 = (f32[1024]{0:T(1024)}, f32[1024]{0:T(1024)S(1)}, u32[]{:S(2)}) copy-start(f32[1024]{0:T(1024)S(1)} %fusion.178) | copy-start | bytes 12292
  865.4 12.0 copy-start.15
  865.4 12.0 copy-start.30
  899.8 10.1 copy-start.34
  928.1 1749.7 %copy-start.21 = (f32[1024]{0:T(1024)S(1)}, f32[1024]{0:T(1024)}, u32[]{:S(2)}) copy-start(f32[1024]{0:T(1024)} %copy-done.20) | copy-start | bytes 12292
  928.2 1749.7 %copy-start.25 = (f32[1024]{0:T(1024)S(1)}, f32[1024]{0:T(1024)}, u32[]{:S(2)}) copy-start(f32[1024]{0:T(1024)} %copy-done.24) | copy-start | bytes 12292
  2684.5 283.0 %reduce-scatter.10.cloned.1.call-start = ((), (), s32[]{:S(2)}) async-start(), calls=%async_computation.15 | async-start | bytes 4325376 | tf_op jit(solution)/shard_map/reduce_scatter | solution.py:262
  2692.1 417.8 %reduce-scatter.12.cloned.1.call-start = ((), (), s32[]{:S(2)}) async-start(), calls=%async_computation.16 | async-start | bytes 4325376 | tf_op jit(solution)/shard_map/reduce_scatter | solution.py:263
  2698.1 553.2 %reduce-scatter.14.cloned.1.call-start = ((), (), s32[]{:S(2)}) async-start(), calls=%async_computation.17 | async-start | bytes 4325376 | tf_op jit(solution)/shard_map/reduce_scatter | solution.py:264
  2705.3 795.8 %reduce-scatter.16.cloned.1.call-start = ((), (), s32[]{:S(2)}) async-start(), calls=%async_computation.18 | async-start | bytes 11894784 | tf_op jit(solution)/shard_map/reduce_scatter | solution.py:266
  2717.3 1036.6 %reduce-scatter.18.cloned.1.call-start = ((), (), s32[]{:S(2)}) async-start(), calls=%async_computation.19 | async-start | bytes 11894784 | tf_op jit(solution)/shard_map/reduce_scatter | solution.py:267
  2729.1 1277.4 %reduce-scatter.20.cloned.1.call-start = ((), (), s32[]{:S(2)}) async-start(), calls=%async_computation.20 | async-start | bytes 11894784 | tf_op jit(solution)/shard_map/reduce_scatter | solution.py:268
  (99 other events, 414.9 us)
Sparse Core Ops, SparseCore 0:
  10.9 59.2 all-gather.7
  73.1 55.3 all-gather.9
  131.3 55.2 all-gather.11
  189.3 55.2 all-gather.13
  247.3 66.1 all-gather.15
  316.2 66.2 all-gather.17
  385.4 66.2 all-gather.19
  2684.6 140.3 reduce-scatter.7
  2827.9 139.6 reduce-scatter.9
  2970.2 139.5 reduce-scatter.11
  3112.7 138.5 reduce-scatter.13
  3254.0 247.0 reduce-scatter.15
  3504.0 249.8 reduce-scatter.17
  3756.6 249.8 reduce-scatter.19
where the time goes:
time: 4060 us; the launch traced here: 4010 us
  local copies, waits for them, and re-layouts  2010 us (50%)
  waiting for transfers between devices  1300 us (32%)
  matrix products  500 us (12%)
  other arithmetic  98.8 us (2%)
  blocking collectives  81.8 us (2%)
    while x320, local copies, waits for them, and re-layouts  768 us
    rev x16, local copies, waits for them, and re-layouts, diagonal_sums(): flipped = matrix[:, ::-1]  419 us
    reshape x16, local copies, waits for them, and re-layouts, build_bias(): return window.reshape(count, length, 2 * length - 1)[:, :, :length]  279 us
    reduce_scatter x1, waiting for transfers between devices, on_device(): lax.psum_scatter(up_term, ('dp', 'fsdp'), scatter_dimension=0, tiled=True)  253 us
    reduce_scatter x1, waiting for transfers between devices, on_device(): lax.psum_scatter(down_term, ('dp', 'fsdp'), scatter_dimension=0, tiled=True)  253 us
    reduce_scatter x1, waiting for transfers between devices, on_device(): lax.psum_scatter(gate_term, ('dp', 'fsdp'), scatter_dimension=0, tiled=True)  250 us
    reshape x16, local copies, waits for them, and re-layouts, diagonal_sums(): return jnp.sum(flat.reshape((length, 2 * length - 1)), axis=0)[::-1]  197 us
    slice x16, local copies, waits for them, and re-layouts, build_bias(): window = flat[:, length - 1:length - 1 + length * (2 * length - 1)]  180 us
  transfers between devices with their start and end apart: 14, of which 9 were waited for; matrix products, arithmetic and copies ran while one was open for 20% of the time, Pallas kernels for 0%

commit v1 on v0

v1 whole, which is shorter than its diff:
```python
import functools

import jax
import jax.numpy as jnp
import numpy as np
from jax import lax
from jax.experimental import pallas as pl
from jax.experimental.pallas import tpu as pltpu
from jax.sharding import PartitionSpec as P

F32 = jnp.float32
BF = jnp.bfloat16
HEADS = 16
BUCKETS = 32
SEQ = 1024
D = 1024
FF = 2816
BLK = 128
NB = SEQ // BLK
STRIP = (2 * NB - 1) * BLK
UNIT = 4
EPS = 1e-06
NEG = -1e30
VLIM = 60 * 1024 * 1024
AXES = ("dp", "fsdp")
GROUP = 512
PIECES = (768, 1024, 1024)
TILE = 256
FT = 256
ANY = pl.BlockSpec(memory_space=pl.ANY)
SMEM = pl.BlockSpec(memory_space=pltpu.SMEM)
HIGHEST = lax.Precision.HIGHEST
GELU_A = 0.7978845608028654
GELU_B = 0.044715


def params(grid=1):
    return pltpu.CompilerParams(vmem_limit_bytes=VLIM, dimension_semantics=("arbitrary",) * grid)


def cost(flops, moved, trans=0):
    return pl.CostEstimate(flops=int(flops), bytes_accessed=int(moved), transcendentals=int(trans))


def nt(a,b): return lax.dot_general(a,b,(((1,),(1,)),((),())),preferred_element_type=F32)
def nn(a,b): return lax.dot_general(a,b,(((1,),(0,)),((),())),preferred_element_type=F32)

def build_strip(rev_ref, strip):
    for h in range(2):
        row=jnp.broadcast_to(rev_ref[h:h+1,:],(8,2*SEQ))
        base=pltpu.roll(row,0,1,stride=1,stride_axis=0)
        for m in range(BLK//8):
            turned=pltpu.roll(base,(8*m-(BLK-1))%(2*SEQ),1)
            for d in range(2*NB-1):
                e=2*NB-2-d
                strip[d*BLK+8*m:d*BLK+8*m+8,h*BLK:(h+1)*BLK]=turned[:,e*BLK:(e+1)*BLK]

def fold_strip(strip, out_ref):
    for h in range(2):
        total=jnp.zeros((8,2*SEQ),F32)
        for m in range(BLK//8):
            parts=[strip[(2*NB-2-e)*BLK+8*m:(2*NB-2-e)*BLK+8*m+8,h*BLK:(h+1)*BLK] for e in range(2*NB-1)]
            parts.append(jnp.zeros((8,BLK),F32))
            total=total+pltpu.roll(jnp.concatenate(parts,axis=1),(BLK-1-8*m)%(2*SEQ),1)
        row=total[0:1]
        for s in range(1,8):
            row=row+pltpu.roll(total[s:s+1],2*SEQ-s,1)
        out_ref[h:h+1,:]=row

def lanes_mask():
    lane=lax.broadcasted_iota(jnp.int32,(1,BLK),1)
    return lane<64

def stack_heads(x, first):
    zero=jnp.zeros_like(x)
    return jnp.concatenate([jnp.where(first,x,zero),jnp.where(first,zero,x)],axis=0)


def strip_kernel(rev_ref, strip):
    build_strip(rev_ref, strip)

def make_strips(rev):
    return pl.pallas_call(strip_kernel,grid=(8,),
        in_specs=[pl.BlockSpec((None,2,2*SEQ),lambda p:(p,0,0))],
        out_specs=pl.BlockSpec((None,STRIP,2*BLK),lambda p:(p,0,0)),
        out_shape=jax.ShapeDtypeStruct((8,STRIP,2*BLK),F32),
        compiler_params=pltpu.CompilerParams(vmem_limit_bytes=VLIM),
        name="bias_strips")(rev)

def attn_fwd_kernel(rng_ref, segk_ref, segq_ref, strip, q_ref, k_ref, v_ref, o_ref, lse_ref, vt):
    first=lanes_mask()
    for u in range(UNIT):
        vt[u]=v_ref[:,u*BLK:(u+1)*BLK].T
    mean=jnp.sum(v_ref[...].astype(F32),axis=0,keepdims=True)*(1.0/SEQ)

    def block(qi, carry):
        q0=pl.multiple_of(qi*BLK,BLK)
        lo=rng_ref[qi]; width=rng_ref[NB+qi]
        k0=pl.multiple_of(lo*BLK,BLK)
        b0=pl.multiple_of((lo-qi+NB-1)*BLK,BLK)
        segq=segq_ref[pl.ds(qi,1),:]
        @pl.when(width==0)
        def _():
            o_ref[pl.ds(q0,BLK),:]=jnp.broadcast_to(mean,(BLK,UNIT*BLK)).astype(BF)
            for u in range(UNIT):
                lse_ref[u,pl.ds(qi,1),:]=jnp.zeros((1,2*BLK),F32)
        for w in range(1,NB+1):
            @pl.when(width==w)
            def _():
                rows=w*BLK
                allowed=segk_ref[pl.ds(k0,rows),:]==segq
                live_row=segq>0
                live_row=jnp.concatenate([live_row,live_row],axis=1)
                live_col=segk_ref[pl.ds(q0,BLK),:]>0
                units=[slice(u*BLK,(u+1)*BLK) for u in range(UNIT)]
                qcats=[stack_heads(q_ref[pl.ds(q0,BLK),lanes],first) for lanes in units]
                scores=[nt(k_ref[pl.ds(k0,rows),lanes],qcat) for lanes,qcat in zip(units,qcats)]
                probs=[]; stats=[]; totals=[]
                for u in range(UNIT):
                    both=[]; stat=[]; tot=[]
                    s=scores[u]+strip[u,pl.ds(b0,rows),:]
                    for h in range(2):
                        sh=jnp.where(allowed,s[:,h*BLK:(h+1)*BLK],NEG)
                        peak=jnp.max(sh,axis=0,keepdims=True)
                        e=jnp.exp(sh-peak)
                        t=jnp.sum(e,axis=0,keepdims=True)
                        both.append(e.astype(BF)); stat.append(peak+jnp.log(t)); tot.append(t)
                    probs.append(jnp.concatenate(both,axis=1)); stats.append(jnp.concatenate(stat,axis=1)); totals.append(jnp.concatenate(tot,axis=1))
                ots=[nn(vt[u,:,pl.ds(k0,rows)],probs[u]) for u in range(UNIT)]
                for u,lanes in enumerate(units):
                    ot=ots[u]*(1.0/totals[u])
                    o=jnp.concatenate([ot[:64,:BLK],ot[64:,BLK:]],axis=0).T
                    o_ref[pl.ds(q0,BLK),lanes]=jnp.where(live_col,o,mean[:,lanes]).astype(BF)
                    lse_ref[u,pl.ds(qi,1),:]=jnp.where(live_row,stats[u],0.0)
        return carry
    lax.fori_loop(0,NB,block,0)

def attn_bwd_kernel(rng_ref, segk_ref, segq_ref, strip, q_ref, k_ref, v_ref, g_ref, lse_ref,
                    dq_ref, dk_ref, dv_ref, off_ref, dstrip, kt, dk, dv):
    first=lanes_mask()
    dstrip[...]=jnp.zeros_like(dstrip)
    dk[...]=jnp.zeros_like(dk)
    for u in range(UNIT):
        lanes=slice(u*BLK,(u+1)*BLK)
        kt[u]=k_ref[:,lanes].T
        padded=jnp.where(segk_ref[...]>0,0.0,g_ref[:,lanes].astype(F32))
        dv[:,lanes]=jnp.broadcast_to(jnp.sum(padded,axis=0,keepdims=True)*(1.0/SEQ),(SEQ,BLK))

    def block(qi, carry):
        q0=pl.multiple_of(qi*BLK,BLK)
        lo=rng_ref[qi]; width=rng_ref[NB+qi]
        k0=pl.multiple_of(lo*BLK,BLK)
        b0=pl.multiple_of((lo-qi+NB-1)*BLK,BLK)
        segq=segq_ref[pl.ds(qi,1),:]
        @pl.when(width==0)
        def _():
            dq_ref[pl.ds(q0,BLK),:]=jnp.zeros((BLK,UNIT*BLK),BF)
        for w in range(1,NB+1):
            @pl.when(width==w)
            def _():
                rows=w*BLK
                allowed=segk_ref[pl.ds(k0,rows),:]==segq
                units=[slice(u*BLK,(u+1)*BLK) for u in range(UNIT)]
                qcats=[stack_heads(q_ref[pl.ds(q0,BLK),lanes],first) for lanes in units]
                gcats=[stack_heads(g_ref[pl.ds(q0,BLK),lanes],first) for lanes in units]
                scores=[nt(k_ref[pl.ds(k0,rows),lanes],qcat) for lanes,qcat in zip(units,qcats)]
                dps=[nt(v_ref[pl.ds(k0,rows),lanes],gcat) for lanes,gcat in zip(units,gcats)]
                probs=[]; grads=[]
                for u in range(UNIT):
                    lse=lse_ref[u,pl.ds(qi,1),:]
                    s=scores[u]+strip[u,pl.ds(b0,rows),:]
                    ps=[]; ds=[]
                    for h in range(2):
                        cols=slice(h*BLK,(h+1)*BLK)
                        prob=jnp.exp(jnp.where(allowed,s[:,cols],NEG)-lse[:,cols])
                        t=prob*dps[u][:,cols]
                        inner=jnp.sum(t,axis=0,keepdims=True)
                        d=t-prob*inner
                        dstrip[u,pl.ds(b0,rows),cols]+=d
                        ps.append(prob.astype(BF)); ds.append(d.astype(BF))
                    probs.append(jnp.concatenate(ps,axis=1)); grads.append(jnp.concatenate(ds,axis=1))
                for u,lanes in enumerate(units):
                    dv[pl.ds(k0,rows),lanes]+=nn(probs[u],gcats[u])
                dqts=[nn(kt[u,:,pl.ds(k0,rows)],grads[u]) for u in range(UNIT)]
                for u,lanes in enumerate(units):
                    dk[pl.ds(k0,rows),lanes]+=nn(grads[u],qcats[u])
                for u,lanes in enumerate(units):
                    dq_ref[pl.ds(q0,BLK),lanes]=jnp.concatenate([dqts[u][:64,:BLK],dqts[u][64:,BLK:]],axis=0).T.astype(BF)
        return carry
    lax.fori_loop(0,NB,block,0)
    dk_ref[...]=dk[...].astype(BF)
    dv_ref[...]=dv[...].astype(BF)
    for u in range(UNIT):
        fold_strip(dstrip.at[u], off_ref.at[u])

def attn_fwd(rng,segk,segq,strips,qkv,pairs,first_pair):
    n=pairs//UNIT; f=first_pair//UNIT; wide=UNIT*BLK
    c=lambda o:pl.BlockSpec((SEQ,wide),lambda p,r:(0,o+p))
    gs=pltpu.PrefetchScalarGridSpec(num_scalar_prefetch=1,grid=(n,),
        in_specs=[pl.BlockSpec((SEQ,BLK),lambda p,r:(0,0)),pl.BlockSpec((NB,BLK),lambda p,r:(0,0)),
                  pl.BlockSpec((UNIT,STRIP,2*BLK),lambda p,r:(f+p,0,0)),
                  c(0),c(n),c(2*n)],
        out_specs=[c(0),pl.BlockSpec((UNIT,NB,2*BLK),lambda p,r:(p,0,0))],
        scratch_shapes=[pltpu.VMEM((UNIT,BLK,SEQ),BF)])
    return pl.pallas_call(attn_fwd_kernel,grid_spec=gs,
        out_shape=[jax.ShapeDtypeStruct((SEQ,pairs*BLK),BF),jax.ShapeDtypeStruct((pairs,NB,2*BLK),F32)],
        compiler_params=pltpu.CompilerParams(vmem_limit_bytes=VLIM,dimension_semantics=("arbitrary",)),
        cost_estimate=pl.CostEstimate(flops=pairs*2*2*SEQ*SEQ*64*4,bytes_accessed=pairs*4*SEQ*BLK*2,transcendentals=pairs*SEQ*SEQ),
        name="attention_forward")(rng,segk,segq,strips,qkv,qkv,qkv)

def attn_bwd(rng,segk,segq,strips,qkv,g,lse,pairs,first_pair):
    n=pairs//UNIT; f=first_pair//UNIT; wide=UNIT*BLK
    c=lambda o:pl.BlockSpec((SEQ,wide),lambda p,r:(0,o+p))
    gs=pltpu.PrefetchScalarGridSpec(num_scalar_prefetch=1,grid=(n,),
        in_specs=[pl.BlockSpec((SEQ,BLK),lambda p,r:(0,0)),pl.BlockSpec((NB,BLK),lambda p,r:(0,0)),
                  pl.BlockSpec((UNIT,STRIP,2*BLK),lambda p,r:(f+p,0,0)),
                  c(0),c(n),c(2*n),c(f),
                  pl.BlockSpec((UNIT,NB,2*BLK),lambda p,r:(p,0,0))],
        out_specs=[c(0),c(0),c(0),pl.BlockSpec((UNIT,2,2*SEQ),lambda p,r:(p,0,0))],
        scratch_shapes=[pltpu.VMEM((UNIT,STRIP,2*BLK),F32),pltpu.VMEM((UNIT,BLK,SEQ),BF),
                        pltpu.VMEM((SEQ,wide),F32),pltpu.VMEM((SEQ,wide),F32)])
    sh=jax.ShapeDtypeStruct((SEQ,pairs*BLK),BF)
    return pl.pallas_call(attn_bwd_kernel,grid_spec=gs,
        out_shape=[sh,sh,sh,jax.ShapeDtypeStruct((pairs,2,2*SEQ),F32)],
        compiler_params=pltpu.CompilerParams(vmem_limit_bytes=VLIM,dimension_semantics=("arbitrary",)),
        cost_estimate=pl.CostEstimate(flops=pairs*5*2*SEQ*SEQ*64*4,bytes_accessed=pairs*8*SEQ*BLK*2,transcendentals=pairs*SEQ*SEQ),
        name="attention_backward")(rng,segk,segq,strips,qkv,qkv,qkv,g,lse)

def ranges(seg):
    s=seg.reshape(NB,BLK)
    least=s[:,0]; most=jnp.max(s,axis=1)
    lo=jnp.sum((most[None,:]<least[:,None])&(least[None,:]>0),axis=1)
    hi=jnp.sum((least[None,:]<=most[:,None])&(least[None,:]>0),axis=1)
    w=jnp.where(least>0,hi-lo,0)
    return jnp.concatenate([jnp.where(least>0,lo,0),w]).astype(jnp.int32)


def shift_blocks(load, src_ref, size):
    per = BLK // size
    lane = lax.broadcasted_iota(jnp.int32, (1, BLK), 1) // size
    for q in range(D // BLK):
        chunk = None
        for t in range(per):
            a = src_ref[q * per + t]
            piece = load(pl.multiple_of((a // per) * BLK, BLK))
            piece = pltpu.roll(piece, lax.rem((t - lax.rem(a, per)) * size + BLK, BLK), 1)
            chunk = piece if chunk is None else jnp.where(lane == t, piece, chunk)
        yield q, chunk


def prep_kernel(size, src_ref, x_ref, c_ref, seg_ref, xo_ref, co_ref, ct_ref):
    live = seg_ref[...] > 0
    for q, chunk in shift_blocks(lambda at: x_ref[:, pl.ds(at, BLK)].astype(F32), src_ref, size):
        xo_ref[:, q * BLK : (q + 1) * BLK] = chunk.astype(BF)
    for q, chunk in shift_blocks(lambda at: c_ref[:, pl.ds(at, BLK)].astype(F32), src_ref, size):
        low = jnp.where(live, chunk, 0.0).astype(BF)
        co_ref[:, q * BLK : (q + 1) * BLK] = low
        ct_ref[q * BLK : (q + 1) * BLK, :] = low.T


def prepare(src, x, c, segk, size):
    rows = TILE
    blk = lambda: pl.BlockSpec((rows, D), lambda i: (i, 0))
    sh = jax.ShapeDtypeStruct((SEQ, D), BF)
    return pl.pallas_call(
        functools.partial(prep_kernel, size),
        grid=(SEQ // rows,),
        in_specs=[SMEM, blk(), blk(), pl.BlockSpec((rows, BLK), lambda i: (i, 0))],
        out_specs=[blk(), blk(), pl.BlockSpec((D, rows), lambda i: (0, i))],
        out_shape=[sh, sh, jax.ShapeDtypeStruct((D, SEQ), BF)],
        compiler_params=params(),
        cost_estimate=cost(0, 10 * SEQ * D),
        name="prepare",
    )(src, x, c, segk)


def block_copies(refs, layout, dst, sems):
    copies = []
    for n, (ref, (row, rows, col, cols, start)) in enumerate(zip(refs, layout)):
        copies.append(
            pltpu.make_async_copy(
                ref.at[:, pl.ds(start, cols)], dst.at[pl.ds(row, rows), pl.ds(col, cols)], sems.at[n]
            )
        )
    return copies


def scaled_rows(x):
    return lax.rsqrt(jnp.mean(x * x, axis=-1, keepdims=True) + EPS)


def qkv_kernel(lead, layout, *refs):
    n = len(layout)
    x_ref, blocks, refs = refs[0], refs[1 : 1 + n], refs[1 + n :]
    if lead:
        out_ref, normed_ref, turned_ref, gains_ref, w, sems = refs
    else:
        out_ref, w, sems = refs

    @pl.when(pl.program_id(0) == 0)
    def _():
        copies = block_copies(blocks, layout, w, sems)
        for c in copies:
            c.start()
        for c in copies:
            c.wait()
        if lead:
            gains_ref[...] = w[:, 3 * GROUP :].astype(F32).T[:8]

    if lead:
        x = x_ref[...].astype(F32)
        normed = (x * scaled_rows(x) * gains_ref[0:1, :]).astype(BF)
        normed_ref[...] = normed
        turned_ref[...] = normed.T
    else:
        normed = x_ref[...]
    for j in range(3):
        cols = slice(j * GROUP, (j + 1) * GROUP)
        out_ref[:, cols] = nn(normed, w[:, cols]).astype(BF)


def project(x, blocks, layout, lead):
    width = 3 * GROUP + (BLK if lead else 0)
    rows = TILE
    tok = lambda c: pl.BlockSpec((rows, c), lambda i: (i, 0))
    out_specs = [tok(3 * GROUP)]
    out_shape = [jax.ShapeDtypeStruct((SEQ, 3 * GROUP), BF)]
    if lead:
        out_specs += [tok(D), pl.BlockSpec((D, rows), lambda i: (0, i)), pl.BlockSpec((8, D), lambda i: (0, 0))]
        out_shape += [
            jax.ShapeDtypeStruct((SEQ, D), BF),
            jax.ShapeDtypeStruct((D, SEQ), BF),
            jax.ShapeDtypeStruct((8, D), F32),
        ]
    return pl.pallas_call(
        functools.partial(qkv_kernel, lead, layout),
        grid=(SEQ // rows,),
        in_specs=[tok(D)] + [ANY] * len(blocks),
        out_specs=out_specs,
        out_shape=out_shape,
        scratch_shapes=[pltpu.VMEM((D, width), BF), pltpu.SemaphoreType.DMA((len(blocks),))],
        compiler_params=params(),
        cost_estimate=cost(2 * SEQ * D * 3 * GROUP, 2 * D * width + 4 * SEQ * D),
        name="query_key_value",
    )(x, *blocks)


def hidden_kernel(layout, *refs):
    n = len(layout)
    a0, a1, x_ref, gains_ref = refs[:4]
    blocks = refs[4 : 4 + n]
    h_ref, n2_ref, n2t_ref, w, sems = refs[4 + n :]

    @pl.when(pl.program_id(0) == 0)
    def _():
        copies = block_copies(blocks, layout, w, sems)
        for c in copies:
            c.start()
        for c in copies:
            c.wait()

    hidden = x_ref[...].astype(F32) + (nt(a0[...], w[:, :GROUP]) + nt(a1[...], w[:, GROUP:]))
    h_ref[...] = hidden
    normed = (hidden * scaled_rows(hidden) * gains_ref[1:2, :]).astype(BF)
    n2_ref[...] = normed
    n2t_ref[...] = normed.T


def hidden_units(a0, a1, x, gains, blocks, layout):
    rows = TILE
    tok = lambda c: pl.BlockSpec((rows, c), lambda i: (i, 0))
    return pl.pallas_call(
        functools.partial(hidden_kernel, layout),
        grid=(SEQ // rows,),
        in_specs=[tok(GROUP), tok(GROUP), tok(D), pl.BlockSpec((8, D), lambda i: (0, 0))] + [ANY] * len(blocks),
        out_specs=[tok(D), tok(D), pl.BlockSpec((D, rows), lambda i: (0, i))],
        out_shape=[
            jax.ShapeDtypeStruct((SEQ, D), F32),
            jax.ShapeDtypeStruct((SEQ, D), BF),
            jax.ShapeDtypeStruct((D, SEQ), BF),
        ],
        scratch_shapes=[pltpu.VMEM((D, 2 * GROUP), BF), pltpu.SemaphoreType.DMA((len(blocks),))],
        compiler_params=params(),
        cost_estimate=cost(2 * SEQ * D * D, 16 * SEQ * D),
        name="hidden_units",
    )(a0, a1, x, gains, *blocks)


def feed_kernel(lead, width, start, *refs):
    n2, n2t, cot, cott, wlo, whi = refs[:6]
    refs = refs[6:]
    if not lead:
        bo_in, ng_in = refs[:2]
        refs = refs[2:]
    keep, send, bo_out, ng_out = refs[:4]
    n2_v, n2t_v, cot_v, cott_v, w, stage, bo, ng, mix_v, gg_v, ug_v, sem_w, sem_o, sem_i = refs[4:]
    half = D // 2
    tiles = width // FT

    def weight_copies(f):
        out = []
        for j in range(3):
            col = pl.multiple_of(j * width + f * FT, FT)
            for s, src in enumerate((wlo, whi)):
                out.append(
                    pltpu.make_async_copy(
                        src.at[:, pl.ds(start + col, FT)],
                        w.at[pl.ds(s * half, half), pl.ds(col, FT)],
                        sem_w.at[f, 2 * j + s],
                    )
                )
        return out

    def term_copies(f):
        out = []
        for j in range(3):
            col = pl.multiple_of(j * width + f * FT, FT)
            for s, dst in enumerate((keep, send)):
                out.append(
                    pltpu.make_async_copy(
                        stage.at[pl.ds(s * half, half), pl.ds(col, FT)],
                        dst.at[:, pl.ds(col, FT)],
                        sem_o.at[f, 2 * j + s],
                    )
                )
        return out

    first = [
        pltpu.make_async_copy(n2, n2_v, sem_i.at[0]),
        pltpu.make_async_copy(cot, cot_v, sem_i.at[1]),
    ]
    second = [
        pltpu.make_async_copy(n2t, n2t_v, sem_i.at[2]),
        pltpu.make_async_copy(cott, cott_v, sem_i.at[3]),
    ]
    if not lead:
        sums_in = [
            pltpu.make_async_copy(bo_in, bo, sem_i.at[4]),
            pltpu.make_async_copy(ng_in, ng, sem_i.at[5]),
        ]
    sums_out = [
        pltpu.make_async_copy(bo, bo_out, sem_i.at[6]),
        pltpu.make_async_copy(ng, ng_out, sem_i.at[7]),
    ]
    for c in weight_copies(0) + first:
        c.start()
    if not lead:
        for c in sums_in:
            c.start()
    for c in second:
        c.start()
    for f in range(1, tiles):
        for c in weight_copies(f):
            c.start()
    if lead:
        bo[...] = jnp.zeros_like(bo)
        ng[...] = jnp.zeros_like(ng)
    for c in first:
        c.wait()

    def step(f, carry):
        for c in weight_copies(f):
            c.wait()
        at = [pl.ds(pl.multiple_of(j * width + f * FT, FT), FT) for j in range(3)]

        def tokens(i, inner):
            rows = pl.ds(pl.multiple_of(i * TILE, TILE), TILE)
            n = n2_v[rows, :]
            gate = nn(n, w[:, at[0]])
            upward = nn(n, w[:, at[1]])
            mixed_grad = nn(cot_v[rows, :], w[:, at[2]])
            square = gate * gate
            bend = jnp.tanh(GELU_A * (gate + GELU_B * (gate * square)))
            curve = 0.5 * (1.0 + bend)
            active = gate * curve
            slope = curve + (0.5 * gate) * (1.0 - bend * bend) * (GELU_A * (1.0 + (3.0 * GELU_B) * square))
            mixed = (active * upward).astype(BF)
            gate_grad = (mixed_grad * upward * slope).astype(BF)
            up_grad = (mixed_grad * active).astype(BF)
            mix_v[rows, :] = mixed
            gg_v[rows, :] = gate_grad
            ug_v[rows, :] = up_grad
            if not lead:

                @pl.when((f == 0) & (i == 0))
                def _():
                    for c in sums_in:
                        c.wait()

            bo[rows, :] += nt(mixed, w[:, at[2]])
            ng[rows, :] += nt(gate_grad, w[:, at[0]]) + nt(up_grad, w[:, at[1]])
            return inner

        lax.fori_loop(0, SEQ // TILE, tokens, 0)

        @pl.when(f == 0)
        def _():
            for c in second:
                c.wait()

        @pl.when(f == tiles - 1)
        def _():
            for c in sums_out:
                c.start()

        def features(i, inner):
            rows = pl.ds(pl.multiple_of(i * TILE, TILE), TILE)
            n = n2t_v[rows, :]
            stage[rows, at[0]] = nn(n, gg_v[...]).astype(BF)
            stage[rows, at[1]] = nn(n, ug_v[...]).astype(BF)
            stage[rows, at[2]] = nn(cott_v[rows, :], mix_v[...]).astype(BF)
            return inner

        lax.fori_loop(0, D // TILE, features, 0)
        for c in term_copies(f):
            c.start()
        return carry

    lax.fori_loop(0, tiles, step, 0)
    for c in sums_out:
        c.wait()

    def drain(f, carry):
        for c in term_copies(f):
            c.wait()
        return carry

    lax.fori_loop(0, tiles, drain, 0)


def feed(n2, n2t, cot, cott, blocks, start, width, sums):
    lead = sums is None
    tiles = width // FT
    acts = [n2, n2t, cot, cott, *blocks] + ([] if lead else list(sums))
    half = jax.ShapeDtypeStruct((D // 2, 3 * width), BF)
    total = jax.ShapeDtypeStruct((SEQ, D), F32)
    bf = lambda *s: pltpu.VMEM(s, BF)
    return pl.pallas_call(
        functools.partial(feed_kernel, lead, width, start),
        in_specs=[ANY] * len(acts),
        out_specs=[ANY] * 4,
        out_shape=[half, half, total, total],
        scratch_shapes=[
            bf(SEQ, D), bf(D, SEQ), bf(SEQ, D), bf(D, SEQ), bf(D, 3 * width), bf(D, 3 * width),
            pltpu.VMEM((SEQ, D), F32), pltpu.VMEM((SEQ, D), F32),
            bf(SEQ, FT), bf(SEQ, FT), bf(SEQ, FT),
            pltpu.SemaphoreType.DMA((tiles, 6)), pltpu.SemaphoreType.DMA((tiles, 6)), pltpu.SemaphoreType.DMA((8,)),
        ],
        compiler_params=pltpu.CompilerParams(vmem_limit_bytes=VLIM),
        cost_estimate=cost(9 * 2 * SEQ * D * width, 12 * D * width + 24 * SEQ * D, SEQ * width),
        name="feed_forward",
    )(*acts)


def middle_kernel(layout, *refs):
    n = len(layout)
    h_ref, ng_ref, c_ref, gains_ref = refs[:4]
    blocks = refs[4 : 4 + n]
    hg_ref, bt_ref, ag_ref, gain_ref, w, sems = refs[4 + n :]

    @pl.when(pl.program_id(0) == 0)
    def _():
        copies = block_copies(blocks, layout, w, sems)
        for c in copies:
            c.start()
        for c in copies:
            c.wait()
        gain_ref[...] = jnp.zeros_like(gain_ref)

    hidden = h_ref[...]
    grad = ng_ref[...]
    scale = scaled_rows(hidden)
    gain_ref[0:1, :] += jnp.sum(grad * hidden * scale, axis=0, keepdims=True)
    grad = grad * gains_ref[1:2, :]
    mean = jnp.mean(grad * hidden, axis=-1, keepdims=True)
    out = c_ref[...].astype(F32) + (scale * grad - hidden * (scale * scale * scale * mean))
    hg_ref[...] = out
    low = out.astype(BF)
    bt_ref[...] = low.T
    ag_ref[...] = nn(low, w[...]).astype(BF)


def middle(hidden, ng, cot, gains, blocks, layout):
    rows = TILE
    tok = lambda c: pl.BlockSpec((rows, c), lambda i: (i, 0))
    return pl.pallas_call(
        functools.partial(middle_kernel, layout),
        grid=(SEQ // rows,),
        in_specs=[tok(D), tok(D), tok(D), pl.BlockSpec((8, D), lambda i: (0, 0))] + [ANY] * len(blocks),
        out_specs=[tok(D), pl.BlockSpec((D, rows), lambda i: (0, i)), tok(D), pl.BlockSpec((8, D), lambda i: (0, 0))],
        out_shape=[
            jax.ShapeDtypeStruct((SEQ, D), F32),
            jax.ShapeDtypeStruct((D, SEQ), BF),
            jax.ShapeDtypeStruct((SEQ, D), BF),
            jax.ShapeDtypeStruct((8, D), F32),
        ],
        scratch_shapes=[pltpu.VMEM((D, D), BF), pltpu.SemaphoreType.DMA((len(blocks),))],
        compiler_params=params(),
        cost_estimate=cost(2 * SEQ * D * D, 20 * SEQ * D),
        name="hidden_gradient",
    )(hidden, ng, cot, gains, *blocks)


def terms_kernel(*refs):
    left, rights, (keep, send) = refs[0], refs[1:-2], refs[-2:]
    i = pl.program_id(0)

    def work(out):
        at = 0
        for r in rights:
            wide = r.shape[1]
            out[:, at : at + wide] = nn(left[...], r[...]).astype(BF)
            at += wide

    @pl.when(i < D // TILE // 2)
    def _():
        work(keep)

    @pl.when(i >= D // TILE // 2)
    def _():
        work(send)


def weight_terms(turned, rights):
    width = sum(r.shape[1] for r in rights)
    half = D // TILE // 2
    sh = jax.ShapeDtypeStruct((D // 2, width), BF)
    return pl.pallas_call(
        terms_kernel,
        grid=(D // TILE,),
        in_specs=[pl.BlockSpec((TILE, SEQ), lambda i: (i, 0))]
        + [pl.BlockSpec(r.shape, lambda i: (0, 0)) for r in rights],
        out_specs=[
            pl.BlockSpec((TILE, width), lambda i: (jnp.minimum(i, half - 1), 0)),
            pl.BlockSpec((TILE, width), lambda i: (jnp.maximum(i - half, 0), 0)),
        ],
        out_shape=[sh, sh],
        compiler_params=params(),
        cost_estimate=cost(2 * SEQ * D * width, 4 * SEQ * D + 4 * D * width),
        name="weight_terms",
    )(turned, *rights)


def last_kernel(size, layouts, *refs):
    n = [len(l) for l in layouts]
    back_ref, x_ref, hg_ref, gains_ref = refs[:4]
    grads = refs[4:10]
    blocks = [refs[10 : 10 + n[0]], refs[10 + n[0] : 10 + n[0] + n[1]]]
    out_ref, gain_ref, w0, w1, scratch, sem0, sem1 = refs[10 + n[0] + n[1] :]

    @pl.when(pl.program_id(0) == 0)
    def _():
        copies = block_copies(blocks[0], layouts[0], w0, sem0) + block_copies(blocks[1], layouts[1], w1, sem1)
        for c in copies:
            c.start()
        for c in copies:
            c.wait()
        gain_ref[...] = jnp.zeros_like(gain_ref)

    grad = None
    for g, w in ((0, w0), (1, w1)):
        for j in range(3):
            part = nt(grads[3 * g + j][...], w[:, j * GROUP : (j + 1) * GROUP])
            grad = part if grad is None else grad + part
    x = x_ref[...].astype(F32)
    scale = scaled_rows(x)
    gain_ref[0:1, :] += jnp.sum(grad * x * scale, axis=0, keepdims=True)
    grad = grad * gains_ref[0:1, :]
    mean = jnp.mean(grad * x, axis=-1, keepdims=True)
    scratch[...] = hg_ref[...] + (scale * grad - x * (scale * scale * scale * mean))
    for q, chunk in shift_blocks(lambda at: scratch[:, pl.ds(at, BLK)], back_ref, size):
        out_ref[:, q * BLK : (q + 1) * BLK] = chunk


def last(back, x, hg, gains, grads, blocks, layouts, size):
    rows = TILE
    tok = lambda c: pl.BlockSpec((rows, c), lambda i: (i, 0))
    return pl.pallas_call(
        functools.partial(last_kernel, size, layouts),
        grid=(SEQ // rows,),
        in_specs=[SMEM, tok(D), tok(D), pl.BlockSpec((8, D), lambda i: (0, 0))]
        + [tok(GROUP)] * 6
        + [ANY] * (len(blocks[0]) + len(blocks[1])),
        out_specs=[tok(D), pl.BlockSpec((8, D), lambda i: (0, 0))],
        out_shape=[jax.ShapeDtypeStruct((SEQ, D), F32), jax.ShapeDtypeStruct((8, D), F32)],
        scratch_shapes=[
            pltpu.VMEM((D, 3 * GROUP), BF), pltpu.VMEM((D, 3 * GROUP), BF), pltpu.VMEM((rows, D), F32),
            pltpu.SemaphoreType.DMA((len(blocks[0]),)), pltpu.SemaphoreType.DMA((len(blocks[1]),)),
        ],
        compiler_params=params(),
        cost_estimate=cost(2 * SEQ * D * 6 * GROUP, 20 * SEQ * D),
        name="input_gradient",
    )(back, x, hg, gains, *grads, *blocks[0], *blocks[1])


def output_plain(size, back_ref, seg_ref, h_ref, bo_ref, out_ref, scratch):
    live = seg_ref[...] > 0
    scratch[...] = h_ref[...] + bo_ref[...]
    for q, chunk in shift_blocks(lambda at: scratch[:, pl.ds(at, BLK)], back_ref, size):
        out_ref[:, q * BLK : (q + 1) * BLK] = jnp.where(live, chunk, 0.0).astype(BF)


def block_output_of(back, segk, hidden, bo, size):
    rows = TILE
    tok = lambda c: pl.BlockSpec((rows, c), lambda i: (i, 0))
    return pl.pallas_call(
        functools.partial(output_plain, size),
        grid=(SEQ // rows,),
        in_specs=[SMEM, tok(BLK), tok(D), tok(D)],
        out_specs=tok(D),
        out_shape=jax.ShapeDtypeStruct((SEQ, D), BF),
        scratch_shapes=[pltpu.VMEM((rows, D), F32)],
        compiler_params=params(),
        cost_estimate=cost(0, 10 * SEQ * D),
        name="block_output",
    )(back, segk, hidden, bo)


def gains_kernel(size, back_ref, one_ref, two_ref, out_ref):
    for j, ref in enumerate((one_ref, two_ref)):
        for q, chunk in shift_blocks(lambda at: ref[:, pl.ds(at, BLK)], back_ref, size):
            out_ref[8 * j + q : 8 * j + q + 1, :] = chunk[0:1]


def natural_gains(back, one, two, size):
    return pl.pallas_call(
        functools.partial(gains_kernel, size),
        in_specs=[SMEM, pl.BlockSpec(memory_space=pltpu.VMEM), pl.BlockSpec(memory_space=pltpu.VMEM)],
        out_specs=pl.BlockSpec(memory_space=pltpu.VMEM),
        out_shape=jax.ShapeDtypeStruct((16, BLK), F32),
        name="gain_terms",
    )(back, one, two)


class Slice:
    def __init__(self, mesh):
        self.count = mesh.shape["dp"] * mesh.shape["fsdp"]
        self.inner = mesh.shape["fsdp"]
        self.core = self.inner
        bits = [1 << b for b in range(self.count.bit_length() - 1)]
        self.rest = [b for b in reversed(bits) if b not in (1, 2, self.core)]
        self.order = [self.core, 2, 1] + self.rest[::-1]
        self.size = D // self.count

    def place(self, index):
        p = index * 0
        for b in self.order:
            p = 2 * p + (index // b) % 2
        return p

    def swap(self, x, bit):
        return lax.ppermute(x, AXES, [(i, i ^ bit) for i in range(self.count)])

    def gather(self, shard, cut):
        line = shard
        for b in self.rest:
            line = jnp.concatenate([line, self.swap(line, b)], axis=0)
        across, along = self.swap(line, 1), self.swap(line, 2)
        low = self.swap(across[:, :cut], 2)
        high = self.swap(along[:, cut:], 1)
        return line, across, along, low, high

    def gather_split(self, shard, cut):
        own = self.gather(shard, cut)
        return own + tuple(self.swap(x, self.core) for x in own)

    def gather_whole(self, shard, cut):
        line, across, along, low, high = self.gather(shard, cut)
        own = jnp.concatenate([line, across, along, jnp.concatenate([low, high], axis=1)], axis=0)
        return own, self.swap(own, self.core)

    def scatter(self, keep, send, cut):
        got = self.swap(send, self.core)
        quarter = D // 8

        def total(r, c):
            rows = slice(r * quarter, (r + 1) * quarter)
            return keep[rows, c].astype(F32) + got[rows, c].astype(F32)

        a, b, both = slice(0, cut), slice(cut, None), slice(None)
        low = self.swap(total(3, a).astype(BF), 2)
        high = self.swap(total(3, b).astype(BF), 1)
        across = jnp.concatenate([total(1, a) + low.astype(F32), total(1, b)], axis=1).astype(BF)
        along = jnp.concatenate([total(2, a), total(2, b) + high.astype(F32)], axis=1).astype(BF)
        line = total(0, both) + self.swap(across, 1).astype(F32) + self.swap(along, 2).astype(F32)
        for bit in self.rest[::-1]:
            half = line.shape[0] // 2
            line = line[:half] + self.swap(line[half:].astype(BF), bit).astype(F32)
        return line

    def sum_all(self, x):
        for bit in self.rest + [1, 2, self.core]:
            x = x + self.swap(x, bit)
        return x


def split_layout(width, cut, used=None):
    used = width if used is None else used
    q = D // 8
    out = []
    for half in range(2):
        at = half * 4 * q
        out += [(at + j * q, q, 0, used, 0) for j in range(3)]
        out += [(at + 3 * q, q, 0, cut, 0), (at + 3 * q, q, cut, used - cut, 0)]
    return tuple(out)


def on_device(
    links,
    layer_input,
    segment_ids,
    relative_buckets,
    first_gain,
    query_weight,
    key_weight,
    value_weight,
    output_projection,
    relative_table,
    second_gain,
    gate_weight,
    up_weight,
    down_projection,
    output_cotangent,
):
    size = links.size
    me = lax.axis_index("dp") * links.inner + lax.axis_index("fsdp")
    place = np.array([links.place(i) for i in range(links.count)], np.int32)
    index = np.argsort(place).astype(np.int32)
    source = jnp.asarray(index) ^ me
    back = jnp.asarray(place) ^ links.place(me)

    gains_shard = jnp.pad(jnp.stack([first_gain, second_gain], axis=1), ((0, 0), (0, BLK - 2)))
    shards = []
    for g in range(2):
        cols = slice(g * GROUP, (g + 1) * GROUP)
        parts = [query_weight[:, cols], key_weight[:, cols], value_weight[:, cols]]
        shards.append(jnp.concatenate(parts + ([gains_shard] if g == 0 else []), axis=1))
    at = 0
    for n, width in enumerate(PIECES):
        cols = slice(at, at + width)
        parts = [gate_weight[:, cols], up_weight[:, cols], down_projection[:, cols]]
        shards.append(jnp.concatenate(([output_projection] if n == 0 else []) + parts, axis=1))
        at += width

    cuts = (7 * BLK, 6 * BLK)
    lead_blocks = links.gather_split(shards[0], cuts[0])
    next_blocks = links.gather_split(shards[1], cuts[1])
    feed_blocks = [links.gather_whole(s, s.shape[1] // 2) for s in shards[2:]]
    layout0 = split_layout(3 * GROUP + BLK, cuts[0])
    layout0_used = split_layout(3 * GROUP + BLK, cuts[0], 3 * GROUP)
    layout1 = split_layout(3 * GROUP, cuts[1])
    layout_o = tuple((s * D // 2, D // 2, 0, D, 0) for s in range(2))

    segk = jnp.broadcast_to(segment_ids[:, None], (SEQ, BLK))
    segq = jnp.where(segment_ids > 0, segment_ids, -1).reshape(NB, BLK)
    spans = ranges(segment_ids)
    one_hot = (relative_buckets[::-1][:, None] == jnp.arange(BUCKETS)[None, :]).astype(BF)
    one_hot = jnp.pad(one_hot, ((0, 1), (0, 0)))
    offsets = lax.dot_general(relative_table, one_hot, (((0,), (1,)), ((), ())), preferred_element_type=F32)
    strips = make_strips(offsets.reshape(HEADS // 2, 2, 2 * SEQ))
    x, cot, cott = prepare(source, layer_input, output_cotangent, segk, size)

    qkv0, normed, turned, gains = project(x, lead_blocks, layout0, True)
    att0, lse0 = attn_fwd(spans, segk, segq, strips, qkv0, 4, 0)
    (qkv1,) = project(normed, next_blocks, layout1, False)
    att1, lse1 = attn_fwd(spans, segk, segq, strips, qkv1, 4, 4)
    hidden, n2, n2t = hidden_units(att0, att1, x, gains, feed_blocks[0], layout_o)

    sums = None
    feed_terms = []
    for n, width in enumerate(PIECES):
        keep, send, bo, ng = feed(n2, n2t, cot, cott, feed_blocks[n], D if n == 0 else 0, width, sums)
        sums = (bo, ng)
        feed_terms.append(links.scatter(keep, send, keep.shape[1] // 2))
    block_output = block_output_of(back, segk, hidden, bo, size)
    hidden_grad, branch_t, attended_grad, second_term = middle(hidden, ng, cot, gains, feed_blocks[0], layout_o)

    grads0 = attn_bwd(spans, segk, segq, strips, qkv0, attended_grad, lse0, 4, 0)
    keep_o, send_o = weight_terms(branch_t, [att0, att1])
    keep0, send0 = weight_terms(turned, grads0[:3])
    term_o = links.scatter(keep_o, send_o, D // 2)
    term0 = links.scatter(keep0, send0, 6 * BLK)
    grads1 = attn_bwd(spans, segk, segq, strips, qkv1, attended_grad, lse1, 4, 4)
    keep1, send1 = weight_terms(turned, grads1[:3])
    term1 = links.scatter(keep1, send1, 6 * BLK)
    input_gradient, first_term = last(
        back, x, hidden_grad, gains, [*grads0[:3], *grads1[:3]], [lead_blocks, next_blocks], [layout0_used, layout1], size
    )
    offset_grads = jnp.concatenate([grads0[3], grads1[3]], axis=0).reshape(HEADS, 2 * SEQ)
    table_term = lax.dot_general(
        one_hot.astype(F32), offset_grads, (((0,), (1,)), ((), ())), precision=HIGHEST, preferred_element_type=F32
    )
    small = jnp.concatenate(
        [natural_gains(back, first_term, second_term, size), table_term.reshape(-1, BLK), jnp.zeros((4, BLK), F32)], axis=0
    )
    small = links.sum_all(small)
    gain_sums = small[:16].reshape(2, D)
    mine = lax.dynamic_slice_in_dim(gain_sums, me * size, size, 1)
    table_gradient = small[16:20].reshape(BUCKETS, HEADS)

    qkv_grads = [
        jnp.concatenate([term0[:, j * GROUP : (j + 1) * GROUP], term1[:, j * GROUP : (j + 1) * GROUP]], axis=1)
        for j in range(3)
    ]
    feed_grads = [
        jnp.concatenate([t[:, j * w : (j + 1) * w] for t, w in zip(feed_terms, PIECES)], axis=1) for j in range(3)
    ]
    return (
        block_output,
        input_gradient,
        *qkv_grads,
        term_o,
        *feed_grads,
        mine[0],
        mine[1],
        table_gradient,
    )


def solution(mesh):
    rows, flat, full = P(AXES, None), P(AXES), P()
    return jax.shard_map(
        functools.partial(on_device, Slice(mesh)),
        mesh=mesh,
        in_specs=(rows, flat, full, flat, rows, rows, rows, rows, full, flat, rows, rows, rows, rows),
        out_specs=(rows,) * 9 + (flat, flat, full),
        check_vma=False,
    )
```

time: 4060 us -> 697 us (0.17)
  local copies, waits for them, and re-layouts: 2010 us -> 37.6 us
  waiting for transfers between devices: 1300 us -> 185 us
  matrix products: 500 us -> 1.54 us
  Pallas kernels: 0 us -> 301 us
  starting transfers between devices: 0.56 us -> 104 us
  blocking collectives: 81.8 us -> 0 us
  other arithmetic: 98.8 us -> 51.6 us
    reduce_scatter x7 -> x0, waiting for transfers between devices: 1190 us -> none  [the longest x1 253 us: on_device(): lax.psum_scatter(up_term, ('dp', 'fsdp'), scatter_dimension=0, tiled=True)]
    while x320 -> x0, local copies, waits for them, and re-layouts: 768 us -> none
    dot_general x134 -> x2, matrix products: 500 us -> 1.54 us  [the longest x1 0.97 us: on_device(): lax.dot_general(relative_table, one_hot, (((0,), (1,)), ((), ())), prefer...]
    reshape x32 -> x5, local copies, waits for them, and re-layouts: 476 us -> 2.5 us  [the longest x1 1.63 us: on_device(): strips = make_strips(offsets.reshape(HEADS // 2, 2, 2 * SEQ))]
    rev x16 -> x0, local copies, waits for them, and re-layouts: 419 us -> none  [diagonal_sums(): flipped = matrix[:, ::-1]]
    pallas_call x0 -> x19, Pallas kernels: none -> 301 us  [the longest x3 111 us: feed(): pl.pallas_call(functools.partial(feed_kernel, lead, width, start), in_spe...]
    slice x48 -> x37, local copies, waits for them, and re-layouts: 302 us -> 12.3 us  [the longest x5 3.41 us: on_device(): parts = [gate_weight[:, cols], up_weight[:, cols], down_projection[:, cols]]]
    ppermute x0 -> x90, waiting for transfers between devices: none -> 185 us  [swap(): return lax.ppermute(x, AXES, [(i, i ^ bit) for i in range(self.count)])]
  transfers between devices with their start and end apart: 14 -> 90, of which waited for: 9 -> 35; matrix products, arithmetic and copies ran while one was open for 20% -> 12% of each run, Pallas kernels for 0% -> 28%
where the time goes in v1:
time: 697 us; the launch traced here: 684 us
  Pallas kernels  301 us (43%)
  waiting for transfers between devices  185 us (27%)
  starting transfers between devices  104 us (15%)
  other arithmetic  51.6 us (7%)
  local copies, waits for them, and re-layouts  37.6 us (5%)
    ppermute x90, waiting for transfers between devices, swap(): return lax.ppermute(x, AXES, [(i, i ^ bit) for i in range(self.count)])  185 us
    pallas_call x3, Pallas kernels, feed(): pl.pallas_call(functools.partial(feed_kernel, lead, width, start), in_spe...  111 us
    ppermute x90, starting transfers between devices, swap(): return lax.ppermute(x, AXES, [(i, i ^ bit) for i in range(self.count)])  104 us
    pallas_call x2, Pallas kernels, attn_bwd(): pl.pallas_call(attn_bwd_kernel, grid_spec=gs, out_shape=[sh, sh, sh, jax....  53.1 us
    pallas_call x2, Pallas kernels, attn_fwd(): pl.pallas_call(attn_fwd_kernel, grid_spec=gs, out_shape=[jax.ShapeDtypeSt...  29.1 us
    pallas_call x3, Pallas kernels, weight_terms(): pl.pallas_call(terms_kernel, grid=(D // TILE,), in_specs=[pl.BlockSpec((T...  21.2 us
    unnamed x143, local copies, waits for them, and re-layouts  19.8 us
    pallas_call x1, Pallas kernels, last(): pl.pallas_call(functools.partial(last_kernel, size, layouts), grid=(SEQ /...  19.6 us
  transfers between devices with their start and end apart: 90, of which 35 were waited for; matrix products, arithmetic and copies ran while one was open for 12% of the time, Pallas kernels for 28%

profile of v1, /device:TPU:0, one launch (start us, length us, event | category | flops | bytes accessed | tf_op | source)
XLA Modules:
  0.0 683.6 jit_solution(3234787827242028635)
XLA Ops:
  30.5 9.8 %bias_strips.1.strip = f32[8,1920,256]{2,1,0:T(8,128)} custom-call(f32[8,2,2048]{2,1,0:T(2,128)} %reshape.59.rev_ref), custom_call_target="tpu_custom_call" | custom-call | tf_op jit(solution)/shard_map/bias_strips/pallas_call | solution.py:83
  44.7 10.7 %prepare.1 = (bf16[1024,1024]{1,0:T(8,128)(2,1)}, bf16[1024,1024]{1,0:T(8,128)(2,1)}, bf16[1024,1024]{1,0:T(8,128)(2,1)}) custom-call(s32[32]{0:T(128)} %broadcast_xor_fusion.src_ref, bf16[1024,1024]{1,0:T(8,128)(2,1)} %x_ref.1, bf16[1024,1024]{1,0:T(8,128)(2,1)} %c_ref.1, s32[1024,128]{1,0:T(8,128)} %broadcast_in_dim.11.seg_ref.segk_ref), custom_call_target="tpu_custom_call" | custom-call | bytes 10485760 | tf_op jit(solution)/shard_map/prepare/pallas_call | solution.py:265
  82.0 11.1 %collective-permute-done.23 = bf16[64,3328]{1,0:T(8,128)(2,1)S(1)} collective-permute-done((bf16[64,3328]{1,0:T(8,128)(2,1)S(1)}, bf16[64,3328]{1,0:T(8,128)(2,1)S(1)}, u32[]{:S(2)}, u32[]{:S(2)}) %collective-permute-start.23) | collective-permute-done | bytes 426016 | tf_op jit(solution)/shard_map/ppermute | solution.py:752
  107.5 18.0 %collective-permute-done.15.refs_4_.refs_23_ = bf16[128,768]{1,0:T(8,128)(2,1)S(1)} collective-permute-done((bf16[128,768]{1,0:T(8,128)(2,1)S(1)}, bf16[128,768]{1,0:T(8,128)(2,1)S(1)}, u32[]{:S(2)}, u32[]{:S(2)}) %collective-permute-start.15) | collective-permute-done | bytes 196640 | tf_op jit(solution)/shard_map/ppermute | solution.py:752
  137.5 8.4 %collective-permute-done.26 = bf16[128,1664]{1,0:T(8,128)(2,1)S(1)} collective-permute-done((bf16[128,1664]{1,0:T(8,128)(2,1)S(1)}, bf16[128,1664]{1,0:T(8,128)(2,1)S(1)}, u32[]{:S(2)}, u32[]{:S(2)}) %collective-permute-start.26) | collective-permute-done | bytes 426016 | tf_op jit(solution)/shard_map/ppermute | solution.py:752
  148.8 8.9 %query_key_value.2 = (bf16[1024,1536]{1,0:T(8,128)(2,1)}, bf16[1024,1024]{1,0:T(8,128)(2,1)}, bf16[1024,1024]{1,0:T(8,128)(2,1)}, f32[8,1024]{1,0:T(8,128)}) custom-call(bf16[1024,1024]{1,0:T(8,128)(2,1)} %get-tuple-element.58.refs_0_.refs_2_.refs_1_, bf16[128,1664]{1,0:T(8,128)(2,1)} %copy-done.39, bf16[128,1664]{1,0:T(8,128)(2,1)} %copy-done.42, ...), custom_call_target="tpu_custom_call" | custom-call | flops 3221225472 | bytes 7602176 | tf_op jit(solution)/shard_map/query_key_value/pallas_call | solution.py:335
  160.6 8.3 %query_key_value.3.q_ref.k_ref.v_ref = bf16[1024,1536]{1,0:T(8,128)(2,1)} custom-call(bf16[1024,1024]{1,0:T(8,128)(2,1)} %get-tuple-element.61.refs_0_, bf16[128,1536]{1,0:T(8,128)(2,1)} %copy-done.40, bf16[128,1536]{1,0:T(8,128)(2,1)} %collective-permute-done.13.refs_2_.refs_21_, bf16[128,1536]{1,0:T(8,128)(2,1)} %collective-permute-done.14.refs_3_.refs_22_, ...), custom_call_target="tpu_custom_call" | custom-call | flops 3221225472 | bytes 7340032 | tf_op jit(solution)/shard_map/query_key_value/pallas_call | solution.py:335
  176.4 10.9 %collective-permute-done.40 = bf16[128,1536]{1,0:T(8,128)(2,1)S(1)} collective-permute-done((bf16[128,1536]{1,0:T(8,128)(2,1)S(1)}, bf16[128,1536]{1,0:T(8,128)(2,1)S(1)}, u32[]{:S(2)}, u32[]{:S(2)}) %collective-permute-start.40) | collective-permute-done | bytes 393248 | tf_op jit(solution)/shard_map/ppermute | solution.py:752
  188.9 14.6 %attention_forward.3 = (bf16[1024,512]{1,0:T(8,128)(2,1)}, f32[4,8,256]{2,1,0:T(8,128)}) custom-call(s32[16]{0:T(128)} %pad_add_fusion.rng_ref, s32[1024,128]{1,0:T(8,128)} %broadcast_in_dim.11.seg_ref.segk_ref, s32[8,128]{1,0:T(8,128)} %fusion.2.segq_ref, f32[8,1920,256]{2,1,0:T(8,128)} %bias_strips.1.strip, ...), custom_call_target="tpu_custom_call" | custom-call | flops 4294967296 | bytes 4194304 | tf_op jit(solution)/shard_map/attention_forward/pallas_call | solution.py:205
  203.5 14.4 %attention_forward.2 = (bf16[1024,512]{1,0:T(8,128)(2,1)}, f32[4,8,256]{2,1,0:T(8,128)}) custom-call(s32[16]{0:T(128)} %pad_add_fusion.rng_ref, s32[1024,128]{1,0:T(8,128)} %broadcast_in_dim.11.seg_ref.segk_ref, s32[8,128]{1,0:T(8,128)} %fusion.2.segq_ref, f32[8,1920,256]{2,1,0:T(8,128)} %bias_strips.1.strip, ...), custom_call_target="tpu_custom_call" | custom-call | flops 4294967296 | bytes 4194304 | tf_op jit(solution)/shard_map/attention_forward/pallas_call | solution.py:205
  235.4 9.2 %hidden_units.1 = (f32[1024,1024]{1,0:T(8,128)}, bf16[1024,1024]{1,0:T(8,128)(2,1)}, bf16[1024,1024]{1,0:T(8,128)(2,1)}) custom-call(bf16[1024,512]{1,0:T(8,128)(2,1)} %get-tuple-element.60.refs_0_.refs_1_, bf16[1024,512]{1,0:T(8,128)(2,1)} %get-tuple-element.62.refs_1_.refs_2_, bf16[1024,1024]{1,0:T(8,128)(2,1)} %get-tuple-element.58.refs_0_.refs_2_.refs_1_, ...), custom_call_target="tpu_custom_call" | custom-call | flops 2147483648 | bytes 16777216 | tf_op jit(solution)/shard_map/hidden_units/pallas_call | solution.py:372
  244.6 27.0 %feed_forward.3 = (bf16[512,2304]{1,0:T(8,128)(2,1)}, bf16[512,2304]{1,0:T(8,128)(2,1)}, f32[1024,1024]{1,0:T(8,128)}, f32[1024,1024]{1,0:T(8,128)}) custom-call(bf16[1024,1024]{1,0:T(8,128)(2,1)} %get-tuple-element.65.refs_0_, bf16[1024,1024]{1,0:T(8,128)(2,1)} %get-tuple-element.66.refs_1_, bf16[1024,1024]{1,0:T(8,128)(2,1)} %get-tuple-element.67.refs_2_, ...), custom_call_target="tpu_custom_call" | custom-call | flops 14495514624 | bytes 34603008 | tf_op jit(solution)/shard_map/feed_forward/pallas_call | solution.py:538
  271.6 42.0 %feed_forward.4 = (bf16[512,3072]{1,0:T(8,128)(2,1)}, bf16[512,3072]{1,0:T(8,128)(2,1)}, f32[1024,1024]{1,0:T(8,128)}, f32[1024,1024]{1,0:T(8,128)}) custom-call(bf16[1024,1024]{1,0:T(8,128)(2,1)} %get-tuple-element.65.refs_0_, bf16[1024,1024]{1,0:T(8,128)(2,1)} %get-tuple-element.66.refs_1_, bf16[1024,1024]{1,0:T(8,128)(2,1)} %get-tuple-element.67.refs_2_, ...), custom_call_target="tpu_custom_call" | custom-call | flops 19327352832 | bytes 37748736 | tf_op jit(solution)/shard_map/feed_forward/pallas_call | solution.py:538
  313.6 42.0 %feed_forward.5 = (bf16[512,3072]{1,0:T(8,128)(2,1)}, bf16[512,3072]{1,0:T(8,128)(2,1)}, f32[1024,1024]{1,0:T(8,128)}, f32[1024,1024]{1,0:T(8,128)}) custom-call(bf16[1024,1024]{1,0:T(8,128)(2,1)} %get-tuple-element.65.refs_0_, bf16[1024,1024]{1,0:T(8,128)(2,1)} %get-tuple-element.66.refs_1_, bf16[1024,1024]{1,0:T(8,128)(2,1)} %get-tuple-element.67.refs_2_, ...), custom_call_target="tpu_custom_call" | custom-call | flops 19327352832 | bytes 37748736 | tf_op jit(solution)/shard_map/feed_forward/pallas_call | solution.py:538
  355.5 10.8 %hidden_gradient.1 = (f32[1024,1024]{1,0:T(8,128)}, bf16[1024,1024]{1,0:T(8,128)(2,1)}, bf16[1024,1024]{1,0:T(8,128)(2,1)}, f32[8,1024]{1,0:T(8,128)}) custom-call(f32[1024,1024]{1,0:T(8,128)} %get-tuple-element.64.h_ref.refs_0_, f32[1024,1024]{1,0:T(8,128)} %get-tuple-element.74.refs_1_, bf16[1024,1024]{1,0:T(8,128)(2,1)} %get-tuple-element.67.refs_2_, ...), custom_call_target="tpu_custom_call" | custom-call | flops 2147483648 | bytes 20971520 | tf_op jit(solution)/shard_map/hidden_gradient/pallas_call | solution.py:586
  366.4 26.3 %attention_backward.3 = (bf16[1024,512]{1,0:T(8,128)(2,1)}, bf16[1024,512]{1,0:T(8,128)(2,1)}, bf16[1024,512]{1,0:T(8,128)(2,1)}, f32[4,2,2048]{2,1,0:T(2,128)}) custom-call(s32[16]{0:T(128)} %pad_add_fusion.rng_ref, s32[1024,128]{1,0:T(8,128)} %broadcast_in_dim.11.seg_ref.segk_ref, s32[8,128]{1,0:T(8,128)} %fusion.2.segq_ref, ...), custom_call_target="tpu_custom_call" | custom-call | flops 10737418240 | bytes 8388608 | tf_op jit(solution)/shard_map/attention_backward/pallas_call | solution.py:223
  392.6 26.8 %attention_backward.2 = (bf16[1024,512]{1,0:T(8,128)(2,1)}, bf16[1024,512]{1,0:T(8,128)(2,1)}, bf16[1024,512]{1,0:T(8,128)(2,1)}, f32[4,2,2048]{2,1,0:T(2,128)}) custom-call(s32[16]{0:T(128)} %pad_add_fusion.rng_ref, s32[1024,128]{1,0:T(8,128)} %broadcast_in_dim.11.seg_ref.segk_ref, s32[8,128]{1,0:T(8,128)} %fusion.2.segq_ref, ...), custom_call_target="tpu_custom_call" | custom-call | flops 10737418240 | bytes 8388608 | tf_op jit(solution)/shard_map/attention_backward/pallas_call | solution.py:223
  425.6 19.6 %input_gradient.1 = (f32[1024,1024]{1,0:T(8,128)}, f32[8,1024]{1,0:T(8,128)}) custom-call(s32[32]{0:T(128)} %broadcast_xor_fusion.1.back_ref.refs_0_, bf16[1024,1024]{1,0:T(8,128)(2,1)} %get-tuple-element.58.refs_0_.refs_2_.refs_1_, f32[1024,1024]{1,0:T(8,128)} %get-tuple-element.75.refs_2_, f32[8,1024]{1,0:T(8,128)} %get-tuple-element.63.refs_3_, ...), custom_call_target="tpu_custom_call" | custom-call | flops 6442450944 | bytes 20971520 | tf_op jit(solution)/shard_map/input_gradient/pallas_call | solution.py:678
  465.6 7.6 %weight_terms.3 = (bf16[512,1536]{1,0:T(8,128)(2,1)}, bf16[512,1536]{1,0:T(8,128)(2,1)}) custom-call(bf16[1024,1024]{1,0:T(8,128)(2,1)} %get-tuple-element.86.refs_0_, bf16[1024,512]{1,0:T(8,128)(2,1)} %get-tuple-element.78.refs_4_.refs_1_, bf16[1024,512]{1,0:T(8,128)(2,1)} %get-tuple-element.79.refs_5_.refs_2_, ...), custom_call_target="tpu_custom_call" | custom-call | flops 3221225472 | bytes 10485760 | tf_op jit(solution)/shard_map/weight_terms/pallas_call | solution.py:628
  526.4 10.1 %collective-permute-done.46 = bf16[128,768]{1,0:T(8,128)(2,1)S(1)} collective-permute-done((bf16[128,768]{1,0:T(8,128)(2,1)S(1)}, bf16[128,768]{1,0:T(8,128)(2,1)S(1)}, u32[]{:S(2)}, u32[]{:S(2)}) %collective-permute-start.46) | collective-permute-done | bytes 196640 | tf_op jit(solution)/shard_map/ppermute | solution.py:752
  546.0 9.9 %collective-permute-done.47 = bf16[128,1536]{1,0:T(8,128)(2,1)S(1)} collective-permute-done((bf16[128,1536]{1,0:T(8,128)(2,1)S(1)}, bf16[128,1536]{1,0:T(8,128)(2,1)S(1)}, u32[]{:S(2)}, u32[]{:S(2)}) %collective-permute-start.47) | collective-permute-done | bytes 393248 | tf_op jit(solution)/shard_map/ppermute | solution.py:752
  590.2 11.1 %collective-permute-done.68 = bf16[128,2304]{1,0:T(8,128)(2,1)S(1)} collective-permute-done((bf16[128,2304]{1,0:T(8,128)(2,1)S(1)}, bf16[128,2304]{1,0:T(8,128)(2,1)S(1)}, u32[]{:S(2)}, u32[]{:S(2)}) %collective-permute-start.68) | collective-permute-done | bytes 589856 | tf_op jit(solution)/shard_map/ppermute | solution.py:752
  615.6 17.7 %collective-permute-done.74 = bf16[128,1536]{1,0:T(8,128)(2,1)S(1)} collective-permute-done((bf16[128,1536]{1,0:T(8,128)(2,1)S(1)}, bf16[128,1536]{1,0:T(8,128)(2,1)S(1)}, u32[]{:S(2)}, u32[]{:S(2)}) %collective-permute-start.74) | collective-permute-done | bytes 393248 | tf_op jit(solution)/shard_map/ppermute | solution.py:752
  635.1 10.9 %collective-permute-done.81 = bf16[128,1536]{1,0:T(8,128)(2,1)S(1)} collective-permute-done((bf16[128,1536]{1,0:T(8,128)(2,1)S(1)}, bf16[128,1536]{1,0:T(8,128)(2,1)S(1)}, u32[]{:S(2)}, u32[]{:S(2)}) %collective-permute-start.81) | collective-permute-done | bytes 393248 | tf_op jit(solution)/shard_map/ppermute | solution.py:752
  (458 shorter events, 295.6 us)
Async XLA Ops:
  3.8 54.8 %collective-permute-start = (bf16[32,1664]{1,0:T(8,128)(2,1)}, bf16[32,1664]{1,0:T(8,128)(2,1)}, u32[]{:S(2)}, u32[]{:S(2)}) collective-permute-start(bf16[32,1664]{1,0:T(8,128)(2,1)} %pad_maximum_fusion.32), channel_id=1, source_target_pairs={{0,16},{1,17},{2,18},{3,19},{4,20},{5,21},{6,22},{7,23},{8,24},{9,... | collective-permute-start | bytes 319496 | tf_op jit(solution)/shard_map/ppermute | solution.py:752
  8.5 47.6 %collective-permute-start.11 = (bf16[32,1536]{1,0:T(8,128)(2,1)}, bf16[32,1536]{1,0:T(8,128)(2,1)}, u32[]{:S(2)}, u32[]{:S(2)}) collective-permute-start(bf16[32,1536]{1,0:T(8,128)(2,1)} %pad_maximum_fusion.33), channel_id=1, source_target_pairs={{0,16},{1,17},{2,18},{3,19},{4,20},{5,21},{6,22},{7,23},{8,24},{9,... | collective-permute-start | bytes 294920 | tf_op jit(solution)/shard_map/ppermute | solution.py:752
  12.6 54.9 %collective-permute-start.22 = (bf16[32,3328]{1,0:T(8,128)(2,1)}, bf16[32,3328]{1,0:T(8,128)(2,1)}, u32[]{:S(2)}, u32[]{:S(2)}) collective-permute-start(bf16[32,3328]{1,0:T(8,128)(2,1)} %get-tuple-element.199), channel_id=1, source_target_pairs={{0,16},{1,17},{2,18},{3,19},{4,20},{5,21},{6,22},{7,23},{8,24},{9,... | collective-permute-start | bytes 638984 | tf_op jit(solution)/shard_map/ppermute | solution.py:752
  17.4 42.7 %collective-permute-start.36 = (bf16[32,3072]{1,0:T(8,128)(2,1)}, bf16[32,3072]{1,0:T(8,128)(2,1)}, u32[]{:S(2)}, u32[]{:S(2)}) collective-permute-start(bf16[32,3072]{1,0:T(8,128)(2,1)} %get-tuple-element.207), channel_id=1, source_target_pairs={{0,16},{1,17},{2,18},{3,19},{4,20},{5,21},{6,22},{7,23},{8,24},{9,... | collective-permute-start | bytes 589832 | tf_op jit(solution)/shard_map/ppermute | solution.py:752
  18.2 44.5 %collective-permute-start.29 = (bf16[32,3072]{1,0:T(8,128)(2,1)}, bf16[32,3072]{1,0:T(8,128)(2,1)}, u32[]{:S(2)}, u32[]{:S(2)}) collective-permute-start(bf16[32,3072]{1,0:T(8,128)(2,1)} %get-tuple-element.209), channel_id=1, source_target_pairs={{0,16},{1,17},{2,18},{3,19},{4,20},{5,21},{6,22},{7,23},{8,24},{9,... | collective-permute-start | bytes 589832 | tf_op jit(solution)/shard_map/ppermute | solution.py:752
  63.7 31.9 %collective-permute-start.30 = (bf16[64,3072]{1,0:T(8,128)(2,1)S(1)}, bf16[64,3072]{1,0:T(8,128)(2,1)S(1)}, u32[]{:S(2)}, u32[]{:S(2)}) collective-permute-start(bf16[64,3072]{1,0:T(8,128)(2,1)S(1)} %pad_maximum_fusion.12), channel_id=1, source_target_pairs={{0,8},{1,9},{2,10},{3,11},{4,12},{5,13},{6,14},{7,15},{8,0},{9,1},... | collective-permute-start | bytes 1179656 | tf_op jit(solution)/shard_map/ppermute | solution.py:752
  95.6 32.9 %collective-permute-start.24 = (bf16[128,3328]{1,0:T(8,128)(2,1)S(1)}, bf16[128,3328]{1,0:T(8,128)(2,1)S(1)}, u32[]{:S(2)}, u32[]{:S(2)}) collective-permute-start(bf16[128,3328]{1,0:T(8,128)(2,1)S(1)} %pad_maximum_fusion), channel_id=1, source_target_pairs={{0,1},{1,0},{2,3},{3,2},{4,5},{5,4},{6,7},{7,6},{8,9},{9,8},{10,11... | collective-permute-start | bytes 2555912 | tf_op jit(solution)/shard_map/ppermute | solution.py:752
  97.2 31.4 %collective-permute-start.25 = (bf16[128,3328]{1,0:T(8,128)(2,1)S(1)}, bf16[128,3328]{1,0:T(8,128)(2,1)S(1)}, u32[]{:S(2)}, u32[]{:S(2)}) collective-permute-start(bf16[128,3328]{1,0:T(8,128)(2,1)S(1)} %pad_maximum_fusion), channel_id=1, source_target_pairs={{0,2},{1,3},{2,0},{3,1},{4,6},{5,7},{6,4},{7,5},{8,10},{9,11},{10,... | collective-permute-start | bytes 2555912 | tf_op jit(solution)/shard_map/ppermute | solution.py:752
  135.5 33.4 %collective-permute-start.38 = (bf16[128,3072]{1,0:T(8,128)(2,1)}, bf16[128,3072]{1,0:T(8,128)(2,1)}, u32[]{:S(2)}, u32[]{:S(2)}) collective-permute-start(bf16[128,3072]{1,0:T(8,128)(2,1)} %pad_maximum_fusion.2), channel_id=1, source_target_pairs={{0,1},{1,0},{2,3},{3,2},{4,5},{5,4},{6,7},{7,6},{8,9},{9,8},{10,11... | collective-permute-start | bytes 2359304 | tf_op jit(solution)/shard_map/ppermute | solution.py:752
  136.3 34.4 %collective-permute-start.39 = (bf16[128,3072]{1,0:T(8,128)(2,1)}, bf16[128,3072]{1,0:T(8,128)(2,1)}, u32[]{:S(2)}, u32[]{:S(2)}) collective-permute-start(bf16[128,3072]{1,0:T(8,128)(2,1)} %pad_maximum_fusion.2), channel_id=1, source_target_pairs={{0,2},{1,3},{2,0},{3,1},{4,6},{5,7},{6,4},{7,5},{8,10},{9,11},{10,... | collective-permute-start | bytes 2359304 | tf_op jit(solution)/shard_map/ppermute | solution.py:752
  148.1 87.3 %collective-permute-start.28 = (bf16[512,3328]{1,0:T(8,128)(2,1)S(1)}, bf16[512,3328]{1,0:T(8,128)(2,1)}, u32[]{:S(2)}, u32[]{:S(2)}) collective-permute-start(bf16[512,3328]{1,0:T(8,128)(2,1)S(1)} %maximum_dynamic-update-slice_fusion.refs_4_), channel_id=1, source_target_pairs={{0,4},{1,5},{2,6},{3,7},{4,0},{5,1},{6,2},{7,3},{8,12},{9,13},{10,... | collective-permute-start | bytes 10223624 | tf_op jit(solution)/shard_map/ppermute | solution.py:752
  157.7 60.3 %collective-permute-start.31 = (bf16[128,3072]{1,0:T(8,128)(2,1)}, bf16[128,3072]{1,0:T(8,128)(2,1)}, u32[]{:S(2)}, u32[]{:S(2)}) collective-permute-start(bf16[128,3072]{1,0:T(8,128)(2,1)} %pad_maximum_fusion.1), channel_id=1, source_target_pairs={{0,1},{1,0},{2,3},{3,2},{4,5},{5,4},{6,7},{7,6},{8,9},{9,8},{10,11... | collective-permute-start | bytes 2359304 | tf_op jit(solution)/shard_map/ppermute | solution.py:752
  159.2 59.9 %collective-permute-start.32 = (bf16[128,3072]{1,0:T(8,128)(2,1)}, bf16[128,3072]{1,0:T(8,128)(2,1)}, u32[]{:S(2)}, u32[]{:S(2)}) collective-permute-start(bf16[128,3072]{1,0:T(8,128)(2,1)} %pad_maximum_fusion.1), channel_id=1, source_target_pairs={{0,2},{1,3},{2,0},{3,1},{4,6},{5,7},{6,4},{7,5},{8,10},{9,11},{10,... | collective-permute-start | bytes 2359304 | tf_op jit(solution)/shard_map/ppermute | solution.py:752
  188.9 82.7 %collective-permute-start.42 = (bf16[512,3072]{1,0:T(8,128)(2,1)}, bf16[512,3072]{1,0:T(8,128)(2,1)}, u32[]{:S(2)}, u32[]{:S(2)}) collective-permute-start(bf16[512,3072]{1,0:T(8,128)(2,1)} %maximum_dynamic-update-slice_fusion.2.refs_4_), channel_id=1, source_target_pairs={{0,4},{1,5},{2,6},{3,7},{4,0},{5,1},{6,2},{7,3},{8,12},{9,13},{10,... | collective-permute-start | bytes 9437192 | tf_op jit(solution)/shard_map/ppermute | solution.py:752
  235.1 78.5 %collective-permute-start.35 = (bf16[512,3072]{1,0:T(8,128)(2,1)}, bf16[512,3072]{1,0:T(8,128)(2,1)}, u32[]{:S(2)}, u32[]{:S(2)}) collective-permute-start(bf16[512,3072]{1,0:T(8,128)(2,1)} %maximum_dynamic-update-slice_fusion.1.refs_4_), channel_id=1, source_target_pairs={{0,4},{1,5},{2,6},{3,7},{4,0},{5,1},{6,2},{7,3},{8,12},{9,13},{10,... | collective-permute-start | bytes 9437192 | tf_op jit(solution)/shard_map/ppermute | solution.py:752
  425.6 49.0 %collective-permute-start.57 = (bf16[512,1024]{1,0:T(8,128)(2,1)}, bf16[512,1024]{1,0:T(8,128)(2,1)S(1)}, u32[]{:S(2)}, u32[]{:S(2)}) collective-permute-start(bf16[512,1024]{1,0:T(8,128)(2,1)} %get-tuple-element.93), channel_id=1, source_target_pairs={{0,4},{1,5},{2,6},{3,7},{4,0},{5,1},{6,2},{7,3},{8,12},{9,13},{10,... | collective-permute-start | bytes 3145736 | tf_op jit(solution)/shard_map/ppermute | solution.py:752
  473.2 36.1 %collective-permute-start.43 = (bf16[512,1536]{1,0:T(8,128)(2,1)}, bf16[512,1536]{1,0:T(8,128)(2,1)}, u32[]{:S(2)}, u32[]{:S(2)}) collective-permute-start(bf16[512,1536]{1,0:T(8,128)(2,1)} %get-tuple-element.88), channel_id=1, source_target_pairs={{0,4},{1,5},{2,6},{3,7},{4,0},{5,1},{6,2},{7,3},{8,12},{9,13},{10,... | collective-permute-start | bytes 4718600 | tf_op jit(solution)/shard_map/ppermute | solution.py:752
  484.4 59.4 %collective-permute-start.64 = (bf16[512,2304]{1,0:T(8,128)(2,1)}, bf16[512,2304]{1,0:T(8,128)(2,1)S(1)}, u32[]{:S(2)}, u32[]{:S(2)}) collective-permute-start(bf16[512,2304]{1,0:T(8,128)(2,1)} %get-tuple-element.95), channel_id=1, source_target_pairs={{0,4},{1,5},{2,6},{3,7},{4,0},{5,1},{6,2},{7,3},{8,12},{9,13},{10,... | collective-permute-start | bytes 7077896 | tf_op jit(solution)/shard_map/ppermute | solution.py:752
  504.8 83.0 %collective-permute-start.71 = (bf16[512,3072]{1,0:T(8,128)(2,1)}, bf16[512,3072]{1,0:T(8,128)(2,1)S(1)}, u32[]{:S(2)}, u32[]{:S(2)}) collective-permute-start(bf16[512,3072]{1,0:T(8,128)(2,1)} %get-tuple-element.97), channel_id=1, source_target_pairs={{0,4},{1,5},{2,6},{3,7},{4,0},{5,1},{6,2},{7,3},{8,12},{9,13},{10,... | collective-permute-start | bytes 9437192 | tf_op jit(solution)/shard_map/ppermute | solution.py:752
  508.0 80.0 %collective-permute-start.78 = (bf16[512,3072]{1,0:T(8,128)(2,1)}, bf16[512,3072]{1,0:T(8,128)(2,1)S(1)}, u32[]{:S(2)}, u32[]{:S(2)}) collective-permute-start(bf16[512,3072]{1,0:T(8,128)(2,1)} %get-tuple-element.99), channel_id=1, source_target_pairs={{0,4},{1,5},{2,6},{3,7},{4,0},{5,1},{6,2},{7,3},{8,12},{9,13},{10,... | collective-permute-start | bytes 9437192 | tf_op jit(solution)/shard_map/ppermute | solution.py:752
  606.0 41.7 %collective-permute-start.73 = (bf16[128,3072]{1,0:T(8,128)(2,1)S(1)}, bf16[128,3072]{1,0:T(8,128)(2,1)S(1)}, u32[]{:S(2)}, u32[]{:S(2)}) collective-permute-start(bf16[128,3072]{1,0:T(8,128)(2,1)S(1)} %pad_maximum_fusion.3), channel_id=1, source_target_pairs={{0,1},{1,0},{2,3},{3,2},{4,5},{5,4},{6,7},{7,6},{8,9},{9,8},{10,11... | collective-permute-start | bytes 2359304 | tf_op jit(solution)/shard_map/ppermute | solution.py:752
  610.3 42.4 %collective-permute-start.80 = (bf16[128,3072]{1,0:T(8,128)(2,1)S(1)}, bf16[128,3072]{1,0:T(8,128)(2,1)S(1)}, u32[]{:S(2)}, u32[]{:S(2)}) collective-permute-start(bf16[128,3072]{1,0:T(8,128)(2,1)S(1)} %pad_maximum_fusion.5), channel_id=1, source_target_pairs={{0,1},{1,0},{2,3},{3,2},{4,5},{5,4},{6,7},{7,6},{8,9},{9,8},{10,11... | collective-permute-start | bytes 2359304 | tf_op jit(solution)/shard_map/ppermute | solution.py:752
  611.9 34.0 %collective-permute-start.81 = (bf16[128,1536]{1,0:T(8,128)(2,1)S(1)}, bf16[128,1536]{1,0:T(8,128)(2,1)S(1)}, u32[]{:S(2)}, u32[]{:S(2)}) collective-permute-start(bf16[128,1536]{1,0:T(8,128)(2,1)S(1)} %get-tuple-element.171), channel_id=1, source_target_pairs={{0,1},{1,0},{2,3},{3,2},{4,5},{5,4},{6,7},{7,6},{8,9},{9,8},{10,11... | collective-permute-start | bytes 1179656 | tf_op jit(solution)/shard_map/ppermute | solution.py:752
  612.4 35.3 %collective-permute-start.70 = (bf16[32,2304]{1,0:T(8,128)(2,1)S(1)}, bf16[32,2304]{1,0:T(8,128)(2,1)S(1)}, u32[]{:S(2)}, u32[]{:S(2)}) collective-permute-start(bf16[32,2304]{1,0:T(8,128)(2,1)S(1)} %slice.836), channel_id=1, source_target_pairs={{0,16},{1,17},{2,18},{3,19},{4,20},{5,21},{6,22},{7,23},{8,24},{9,... | collective-permute-start | bytes 442376 | tf_op jit(solution)/shard_map/ppermute | solution.py:752
  (130 other events, 1634.9 us)

commit v2 on v1

v2 whole, which is shorter than its diff:
```python
import functools

import jax
import jax.numpy as jnp
import numpy as np
from jax import lax
from jax.experimental import pallas as pl
from jax.experimental.pallas import tpu as pltpu
from jax.sharding import PartitionSpec as P

F32 = jnp.float32
BF = jnp.bfloat16
HEADS = 16
BUCKETS = 32
SEQ = 1024
D = 1024
FF = 2816
BLK = 128
NB = SEQ // BLK
STRIP = (2 * NB - 1) * BLK
EPS = 1e-06
NEG = -1e30
VLIM = 60 * 1024 * 1024
AXES = ("dp", "fsdp")
GROUP = 512
PIECES = (768, 1024, 1024)
TILE = 512
FT = 256
ANY = pl.BlockSpec(memory_space=pl.ANY)
SMEM = pl.BlockSpec(memory_space=pltpu.SMEM)
HIGHEST = lax.Precision.HIGHEST
RATE = 1e9
GELU_A = 0.7978845608028654
GELU_B = 0.044715


def params(grid=1):
    return pltpu.CompilerParams(vmem_limit_bytes=VLIM, dimension_semantics=("arbitrary",) * grid)


def cost(flops, moved, trans=0):
    return pl.CostEstimate(flops=int(flops), bytes_accessed=int(moved), transcendentals=int(trans))


def after(kernel, used, deps):
    if not deps:
        return kernel
    return lambda *refs: kernel(*refs[:used], *refs[used + len(deps) :])


def nt(a,b): return lax.dot_general(a,b,(((1,),(1,)),((),())),preferred_element_type=F32)
def nn(a,b): return lax.dot_general(a,b,(((1,),(0,)),((),())),preferred_element_type=F32)

def build_strip(rev_ref, strip):
    for h in range(2):
        row=jnp.broadcast_to(rev_ref[h:h+1,:],(8,2*SEQ))
        base=pltpu.roll(row,0,1,stride=1,stride_axis=0)
        for m in range(BLK//8):
            turned=pltpu.roll(base,(8*m-(BLK-1))%(2*SEQ),1)
            for d in range(2*NB-1):
                e=2*NB-2-d
                strip[d*BLK+8*m:d*BLK+8*m+8,h*BLK:(h+1)*BLK]=turned[:,e*BLK:(e+1)*BLK]

def fold_strip(strip, out_ref):
    for h in range(2):
        total=jnp.zeros((8,2*SEQ),F32)
        for m in range(BLK//8):
            parts=[strip[(2*NB-2-e)*BLK+8*m:(2*NB-2-e)*BLK+8*m+8,h*BLK:(h+1)*BLK] for e in range(2*NB-1)]
            parts.append(jnp.zeros((8,BLK),F32))
            total=total+pltpu.roll(jnp.concatenate(parts,axis=1),(BLK-1-8*m)%(2*SEQ),1)
        row=total[0:1]
        for s in range(1,8):
            row=row+pltpu.roll(total[s:s+1],2*SEQ-s,1)
        out_ref[h:h+1,:]=row

def lanes_mask():
    lane=lax.broadcasted_iota(jnp.int32,(1,BLK),1)
    return lane<64

def stack_heads(x, first):
    zero=jnp.zeros_like(x)
    return jnp.concatenate([jnp.where(first,x,zero),jnp.where(first,zero,x)],axis=0)


def strip_kernel(rev_ref, strip):
    build_strip(rev_ref, strip)

def make_strips(rev, deps=()):
    return pl.pallas_call(after(strip_kernel, 1, deps),grid=(8,),
        in_specs=[pl.BlockSpec((None,2,2*SEQ),lambda p:(p,0,0))]+[ANY]*len(deps),
        out_specs=pl.BlockSpec((None,STRIP,2*BLK),lambda p:(p,0,0)),
        out_shape=jax.ShapeDtypeStruct((8,STRIP,2*BLK),F32),
        compiler_params=pltpu.CompilerParams(vmem_limit_bytes=VLIM),
        name="bias_strips")(rev, *deps)

def attn_fwd_kernel(UNIT, rng_ref, segk_ref, segq_ref, strip, q_ref, k_ref, v_ref, o_ref, lse_ref, vt):
    first=lanes_mask()
    for u in range(UNIT):
        vt[u]=v_ref[:,u*BLK:(u+1)*BLK].T
    mean=jnp.sum(v_ref[...].astype(F32),axis=0,keepdims=True)*(1.0/SEQ)

    def block(qi, carry):
        q0=pl.multiple_of(qi*BLK,BLK)
        lo=rng_ref[qi]; width=rng_ref[NB+qi]
        k0=pl.multiple_of(lo*BLK,BLK)
        b0=pl.multiple_of((lo-qi+NB-1)*BLK,BLK)
        segq=segq_ref[pl.ds(qi,1),:]
        @pl.when(width==0)
        def _():
            o_ref[pl.ds(q0,BLK),:]=jnp.broadcast_to(mean,(BLK,UNIT*BLK)).astype(BF)
            for u in range(UNIT):
                lse_ref[u,pl.ds(qi,1),:]=jnp.zeros((1,2*BLK),F32)
        for w in range(1,NB+1):
            @pl.when(width==w)
            def _():
                rows=w*BLK
                allowed=segk_ref[pl.ds(k0,rows),:]==segq
                live_row=segq>0
                live_row=jnp.concatenate([live_row,live_row],axis=1)
                live_col=segk_ref[pl.ds(q0,BLK),:]>0
                units=[slice(u*BLK,(u+1)*BLK) for u in range(UNIT)]
                qcats=[stack_heads(q_ref[pl.ds(q0,BLK),lanes],first) for lanes in units]
                scores=[nt(k_ref[pl.ds(k0,rows),lanes],qcat) for lanes,qcat in zip(units,qcats)]
                probs=[]; stats=[]; totals=[]
                for u in range(UNIT):
                    both=[]; stat=[]; tot=[]
                    s=scores[u]+strip[u,pl.ds(b0,rows),:]
                    for h in range(2):
                        sh=jnp.where(allowed,s[:,h*BLK:(h+1)*BLK],NEG)
                        peak=jnp.max(sh,axis=0,keepdims=True)
                        e=jnp.exp(sh-peak)
                        t=jnp.sum(e,axis=0,keepdims=True)
                        both.append(e.astype(BF)); stat.append(peak+jnp.log(t)); tot.append(t)
                    probs.append(jnp.concatenate(both,axis=1)); stats.append(jnp.concatenate(stat,axis=1)); totals.append(jnp.concatenate(tot,axis=1))
                ots=[nn(vt[u,:,pl.ds(k0,rows)],probs[u]) for u in range(UNIT)]
                for u,lanes in enumerate(units):
                    ot=ots[u]*(1.0/totals[u])
                    o=jnp.concatenate([ot[:64,:BLK],ot[64:,BLK:]],axis=0).T
                    o_ref[pl.ds(q0,BLK),lanes]=jnp.where(live_col,o,mean[:,lanes]).astype(BF)
                    lse_ref[u,pl.ds(qi,1),:]=jnp.where(live_row,stats[u],0.0)
        return carry
    lax.fori_loop(0,NB,block,0)

def attn_bwd_kernel(UNIT, rng_ref, segk_ref, segq_ref, strip, q_ref, k_ref, v_ref, g_ref, lse_ref,
                    dq_ref, dk_ref, dv_ref, off_ref, dstrip, kt, dk, dv):
    first=lanes_mask()
    dstrip[...]=jnp.zeros_like(dstrip)
    dk[...]=jnp.zeros_like(dk)
    for u in range(UNIT):
        lanes=slice(u*BLK,(u+1)*BLK)
        kt[u]=k_ref[:,lanes].T
        padded=jnp.where(segk_ref[...]>0,0.0,g_ref[:,lanes].astype(F32))
        dv[:,lanes]=jnp.broadcast_to(jnp.sum(padded,axis=0,keepdims=True)*(1.0/SEQ),(SEQ,BLK))

    def block(qi, carry):
        q0=pl.multiple_of(qi*BLK,BLK)
        lo=rng_ref[qi]; width=rng_ref[NB+qi]
        k0=pl.multiple_of(lo*BLK,BLK)
        b0=pl.multiple_of((lo-qi+NB-1)*BLK,BLK)
        segq=segq_ref[pl.ds(qi,1),:]
        @pl.when(width==0)
        def _():
            dq_ref[pl.ds(q0,BLK),:]=jnp.zeros((BLK,UNIT*BLK),BF)
        for w in range(1,NB+1):
            @pl.when(width==w)
            def _():
                rows=w*BLK
                allowed=segk_ref[pl.ds(k0,rows),:]==segq
                units=[slice(u*BLK,(u+1)*BLK) for u in range(UNIT)]
                qcats=[stack_heads(q_ref[pl.ds(q0,BLK),lanes],first) for lanes in units]
                gcats=[stack_heads(g_ref[pl.ds(q0,BLK),lanes],first) for lanes in units]
                scores=[nt(k_ref[pl.ds(k0,rows),lanes],qcat) for lanes,qcat in zip(units,qcats)]
                dps=[nt(v_ref[pl.ds(k0,rows),lanes],gcat) for lanes,gcat in zip(units,gcats)]
                probs=[]; grads=[]
                for u in range(UNIT):
                    lse=lse_ref[u,pl.ds(qi,1),:]
                    s=scores[u]+strip[u,pl.ds(b0,rows),:]
                    ps=[]; ds=[]
                    for h in range(2):
                        cols=slice(h*BLK,(h+1)*BLK)
                        prob=jnp.exp(jnp.where(allowed,s[:,cols],NEG)-lse[:,cols])
                        t=prob*dps[u][:,cols]
                        inner=jnp.sum(t,axis=0,keepdims=True)
                        d=t-prob*inner
                        dstrip[u,pl.ds(b0,rows),cols]+=d
                        ps.append(prob.astype(BF)); ds.append(d.astype(BF))
                    probs.append(jnp.concatenate(ps,axis=1)); grads.append(jnp.concatenate(ds,axis=1))
                for u,lanes in enumerate(units):
                    dv[pl.ds(k0,rows),lanes]+=nn(probs[u],gcats[u])
                dqts=[nn(kt[u,:,pl.ds(k0,rows)],grads[u]) for u in range(UNIT)]
                for u,lanes in enumerate(units):
                    dk[pl.ds(k0,rows),lanes]+=nn(grads[u],qcats[u])
                for u,lanes in enumerate(units):
                    dq_ref[pl.ds(q0,BLK),lanes]=jnp.concatenate([dqts[u][:64,:BLK],dqts[u][64:,BLK:]],axis=0).T.astype(BF)
        return carry
    lax.fori_loop(0,NB,block,0)
    dk_ref[...]=dk[...].astype(BF)
    dv_ref[...]=dv[...].astype(BF)
    for u in range(UNIT):
        fold_strip(dstrip.at[u], off_ref.at[u])

def attn_fwd(rng, segk, segq, strips, qkv, first_pair, deps=()):
    unit = 4
    wide = unit * BLK
    c = lambda o: pl.BlockSpec((SEQ, wide), lambda p, r: (0, o))
    gs = pltpu.PrefetchScalarGridSpec(
        num_scalar_prefetch=1,
        grid=(1,),
        in_specs=[
            pl.BlockSpec((SEQ, BLK), lambda p, r: (0, 0)),
            pl.BlockSpec((NB, BLK), lambda p, r: (0, 0)),
            pl.BlockSpec((unit, STRIP, 2 * BLK), lambda p, r: (first_pair // unit, 0, 0)),
            c(0), c(1), c(2),
        ] + [ANY] * len(deps),
        out_specs=[c(0), pl.BlockSpec((unit, NB, 2 * BLK), lambda p, r: (0, 0, 0))],
        scratch_shapes=[pltpu.VMEM((unit, BLK, SEQ), BF)],
    )
    return pl.pallas_call(
        after(functools.partial(attn_fwd_kernel, unit), 7, deps),
        grid_spec=gs,
        out_shape=[jax.ShapeDtypeStruct((SEQ, wide), BF), jax.ShapeDtypeStruct((unit, NB, 2 * BLK), F32)],
        compiler_params=params(),
        cost_estimate=cost(13 * RATE, 4 * SEQ * wide * 2),
        name="attention_forward",
    )(rng, segk, segq, strips, qkv, qkv, qkv, *deps)


def attn_bwd(rng, segk, segq, strips, qkv, g, lse, first_pair, deps=()):
    unit = 2
    wide = unit * BLK
    f, l = first_pair // unit, first_pair % 4 // unit
    c = lambda o: pl.BlockSpec((SEQ, wide), lambda p, r: (0, o))
    gs = pltpu.PrefetchScalarGridSpec(
        num_scalar_prefetch=1,
        grid=(1,),
        in_specs=[
            pl.BlockSpec((SEQ, BLK), lambda p, r: (0, 0)),
            pl.BlockSpec((NB, BLK), lambda p, r: (0, 0)),
            pl.BlockSpec((unit, STRIP, 2 * BLK), lambda p, r: (f, 0, 0)),
            c(l), c(2 + l), c(4 + l), c(f),
            pl.BlockSpec((unit, NB, 2 * BLK), lambda p, r: (l, 0, 0)),
        ] + [ANY] * len(deps),
        out_specs=[c(0), c(0), c(0), pl.BlockSpec((unit, 2, 2 * SEQ), lambda p, r: (0, 0, 0))],
        scratch_shapes=[
            pltpu.VMEM((unit, STRIP, 2 * BLK), F32), pltpu.VMEM((unit, BLK, SEQ), BF),
            pltpu.VMEM((SEQ, wide), F32), pltpu.VMEM((SEQ, wide), F32),
        ],
    )
    sh = jax.ShapeDtypeStruct((SEQ, wide), BF)
    return pl.pallas_call(
        after(functools.partial(attn_bwd_kernel, unit), 9, deps),
        grid_spec=gs,
        out_shape=[sh, sh, sh, jax.ShapeDtypeStruct((unit, 2, 2 * SEQ), F32)],
        compiler_params=params(),
        cost_estimate=cost(12 * RATE, 8 * SEQ * wide * 2),
        name="attention_backward",
    )(rng, segk, segq, strips, qkv, qkv, qkv, g, lse, *deps)


def ranges(seg):
    s=seg.reshape(NB,BLK)
    least=s[:,0]; most=jnp.max(s,axis=1)
    lo=jnp.sum((most[None,:]<least[:,None])&(least[None,:]>0),axis=1)
    hi=jnp.sum((least[None,:]<=most[:,None])&(least[None,:]>0),axis=1)
    w=jnp.where(least>0,hi-lo,0)
    return jnp.concatenate([jnp.where(least>0,lo,0),w]).astype(jnp.int32)


def shift_blocks(load, src_ref, size):
    per = BLK // size
    lane = lax.broadcasted_iota(jnp.int32, (1, BLK), 1) // size
    for q in range(D // BLK):
        chunk = None
        for t in range(per):
            a = src_ref[q * per + t]
            piece = load(pl.multiple_of((a // per) * BLK, BLK))
            piece = pltpu.roll(piece, lax.rem((t - lax.rem(a, per)) * size + BLK, BLK), 1)
            chunk = piece if chunk is None else jnp.where(lane == t, piece, chunk)
        yield q, chunk


def prep_kernel(size, src_ref, x_ref, c_ref, seg_ref, xo_ref, co_ref, ct_ref):
    live = seg_ref[...] > 0
    for q, chunk in shift_blocks(lambda at: x_ref[:, pl.ds(at, BLK)].astype(F32), src_ref, size):
        xo_ref[:, q * BLK : (q + 1) * BLK] = chunk.astype(BF)
    for q, chunk in shift_blocks(lambda at: c_ref[:, pl.ds(at, BLK)].astype(F32), src_ref, size):
        low = jnp.where(live, chunk, 0.0).astype(BF)
        co_ref[:, q * BLK : (q + 1) * BLK] = low
        ct_ref[q * BLK : (q + 1) * BLK, :] = low.T


def prepare(src, x, c, segk, size):
    rows = TILE
    blk = lambda: pl.BlockSpec((rows, D), lambda i: (i, 0))
    sh = jax.ShapeDtypeStruct((SEQ, D), BF)
    return pl.pallas_call(
        functools.partial(prep_kernel, size),
        grid=(SEQ // rows,),
        in_specs=[SMEM, blk(), blk(), pl.BlockSpec((rows, BLK), lambda i: (i, 0))],
        out_specs=[blk(), blk(), pl.BlockSpec((D, rows), lambda i: (0, i))],
        out_shape=[sh, sh, jax.ShapeDtypeStruct((D, SEQ), BF)],
        compiler_params=params(),
        cost_estimate=cost(0, 10 * SEQ * D),
        name="prepare",
    )(src, x, c, segk)


def prep_kernel(size, src_ref, x_ref, seg_ref, xo_ref, *turned):
    live = seg_ref[...] > 0
    for q, chunk in shift_blocks(lambda at: x_ref[:, pl.ds(at, BLK)].astype(F32), src_ref, size):
        if turned:
            chunk = jnp.where(live, chunk, 0.0)
        low = chunk.astype(BF)
        xo_ref[:, q * BLK : (q + 1) * BLK] = low
        if turned:
            turned[0][q * BLK : (q + 1) * BLK, :] = low.T


def prepare(src, x, segk, size, masked, deps=()):
    rows = 256
    blk = pl.BlockSpec((rows, D), lambda i: (i, 0))
    out_specs, out_shape = [blk], [jax.ShapeDtypeStruct((SEQ, D), BF)]
    if masked:
        out_specs.append(pl.BlockSpec((D, rows), lambda i: (0, i)))
        out_shape.append(jax.ShapeDtypeStruct((D, SEQ), BF))
    return pl.pallas_call(
        after(functools.partial(prep_kernel, size), 3, deps),
        grid=(SEQ // rows,),
        in_specs=[SMEM, blk, pl.BlockSpec((rows, BLK), lambda i: (i, 0))] + [ANY] * len(deps),
        out_specs=out_specs,
        out_shape=out_shape,
        compiler_params=params(),
        cost_estimate=cost(5 * RATE, 5 * SEQ * D),
        name="prepare",
    )(src, x, segk, *deps)


def pack_kernel(spans, count, *refs):
    ins, outs = refs[:count], refs[count:]
    for out, cols in zip(outs, spans):
        at = 0
        for n, lo, hi in cols:
            out[:, at : at + hi - lo] = ins[n][:, lo:hi]
            at += hi - lo


def pack(shards, spans, deps=()):
    rows = shards[0].shape[0]
    widths = [sum(hi - lo for _, lo, hi in cols) for cols in spans]
    whole = pl.BlockSpec(memory_space=pltpu.VMEM)
    return pl.pallas_call(
        after(functools.partial(pack_kernel, spans, len(shards)), len(shards), deps),
        in_specs=[whole] * len(shards) + [ANY] * len(deps),
        out_specs=[whole] * len(widths),
        out_shape=[jax.ShapeDtypeStruct((rows, w), BF) for w in widths],
        name="pack_shards",
    )(*shards, *deps)


def join(*parts):
    return jnp.concatenate(parts, axis=0)


def add_terms(terms, rows):
    return sum(t[off : off + rows].astype(F32) for t, off in terms).astype(BF)


def finish_kernel(counts, *refs):
    sums, at = [], 0
    for n in counts:
        total = refs[at][...].astype(F32)
        for ref in refs[at + 1 : at + n]:
            total = total + ref[...].astype(F32)
        sums.append(total)
        at += n
    outs = refs[at:]
    for j in range(3):
        outs[j][:, :GROUP] = sums[0][:, D + j * GROUP : D + (j + 1) * GROUP]
        outs[j][:, GROUP:] = sums[1][:, j * GROUP : (j + 1) * GROUP]
    outs[3][...] = sums[0][:, :D]
    at = 0
    for s, width in zip(sums[2:], PIECES):
        for j in range(3):
            outs[4 + j][:, at : at + width] = s[:, j * width : (j + 1) * width]
        at += width


def finish(sets, rows, deps=()):
    flat = [x for terms in sets for x in terms]
    widths = (D,) * 4 + (FF,) * 3
    return pl.pallas_call(
        after(functools.partial(finish_kernel, tuple(len(t) for t in sets)), len(flat), deps),
        grid=(1,),
        in_specs=[pl.BlockSpec((rows, x.shape[1]), lambda i: (0, 0)) for x in flat] + [ANY] * len(deps),
        out_specs=[pl.BlockSpec((rows, w), lambda i: (0, 0)) for w in widths],
        out_shape=[jax.ShapeDtypeStruct((rows, w), F32) for w in widths],
        compiler_params=params(),
        name="weight_gradients",
    )(*flat, *deps)


def layout_of(blocks, order, cols, start=0, at=0):
    q = D // 8
    out = []
    for n, b in enumerate(blocks):
        if b.shape[0] == q:
            out.append((n, n * q, q, at, cols, 0, start))
        else:
            out += [(n, n * 4 * q + p * q, q, at, cols, j * q, start) for j, p in enumerate(order)]
    return tuple(out)


def block_copies(refs, layout, dst, sems, base=0):
    return [
        pltpu.make_async_copy(
            refs[n].at[pl.ds(frm, rows), pl.ds(start, cols)],
            dst.at[pl.ds(row, rows), pl.ds(col, cols)],
            sems.at[base + i],
        )
        for i, (n, row, rows, col, cols, frm, start) in enumerate(layout)
    ]


def fetch(refs, layout, dst, sems):
    copies = block_copies(refs, layout, dst, sems)
    for c in copies:
        c.start()
    for c in copies:
        c.wait()


def scaled_rows(x):
    return lax.rsqrt(jnp.mean(x * x, axis=-1, keepdims=True) + EPS)


def qkv_kernel(lead, layout, count, *refs):
    x_ref, blocks, refs = refs[0], refs[1 : 1 + count], refs[1 + count :]
    if lead:
        out_ref, normed_ref, turned_ref, gains_ref, w, sems = refs
    else:
        out_ref, w, sems = refs
        normed_ref = x_ref
    j = pl.program_id(0)

    @pl.when(j == 0)
    def _():
        fetch(blocks, layout, w, sems)
        if lead:
            gains_ref[...] = w[:, 3 * GROUP :].astype(F32).T[:8]

            def rows_of(i, carry):
                at = pl.multiple_of(i * 256, 256)
                x = x_ref[pl.ds(at, 256), :].astype(F32)
                low = (x * scaled_rows(x) * gains_ref[0:1, :]).astype(BF)
                normed_ref[pl.ds(at, 256), :] = low
                turned_ref[:, pl.ds(at, 256)] = low.T
                return carry

            lax.fori_loop(0, SEQ // 256, rows_of, 0)

    out_ref[...] = nn(normed_ref[...], w[:, pl.ds(pl.multiple_of(j * GROUP, GROUP), GROUP)]).astype(BF)


def project(x, blocks, layout, lead, deps=()):
    width = 3 * GROUP + (BLK if lead else 0)
    whole = lambda r, c: pl.BlockSpec((r, c), lambda j: (0, 0))
    out_specs = [pl.BlockSpec((SEQ, GROUP), lambda j: (0, j))]
    out_shape = [jax.ShapeDtypeStruct((SEQ, 3 * GROUP), BF)]
    if lead:
        out_specs += [whole(SEQ, D), whole(D, SEQ), whole(8, D)]
        out_shape += [
            jax.ShapeDtypeStruct((SEQ, D), BF),
            jax.ShapeDtypeStruct((D, SEQ), BF),
            jax.ShapeDtypeStruct((8, D), F32),
        ]
    n = len(blocks)
    return pl.pallas_call(
        after(functools.partial(qkv_kernel, lead, layout, n), 1 + n, deps),
        grid=(3,),
        in_specs=[whole(SEQ, D)] + [ANY] * (n + len(deps)),
        out_specs=out_specs,
        out_shape=out_shape,
        scratch_shapes=[pltpu.VMEM((D, width), BF), pltpu.SemaphoreType.DMA((len(layout),))],
        compiler_params=params(),
        cost_estimate=cost(6 * RATE, 2 * D * width + 4 * SEQ * D),
        name="query_key_value",
    )(x, *blocks, *deps)


def hidden_kernel(layout, count, *refs):
    a0, a1, x_ref, gains_ref = refs[:4]
    blocks = refs[4 : 4 + count]
    h_ref, n2_ref, n2t_ref, w, sems = refs[4 + count :]

    @pl.when(pl.program_id(0) == 0)
    def _():
        fetch(blocks, layout, w, sems)

    hidden = x_ref[...].astype(F32) + nt(jnp.concatenate([a0[...], a1[...]], axis=1), w[...])
    h_ref[...] = hidden
    normed = (hidden * scaled_rows(hidden) * gains_ref[1:2, :]).astype(BF)
    n2_ref[...] = normed
    n2t_ref[...] = normed.T


def hidden_units(a0, a1, x, gains, blocks, layout, deps=()):
    rows = TILE
    tok = lambda c: pl.BlockSpec((rows, c), lambda i: (i, 0))
    n = len(blocks)
    return pl.pallas_call(
        after(functools.partial(hidden_kernel, layout, n), 4 + n, deps),
        grid=(SEQ // rows,),
        in_specs=[tok(GROUP), tok(GROUP), tok(D), pl.BlockSpec((8, D), lambda i: (0, 0))] + [ANY] * (n + len(deps)),
        out_specs=[tok(D), tok(D), pl.BlockSpec((D, rows), lambda i: (0, i))],
        out_shape=[
            jax.ShapeDtypeStruct((SEQ, D), F32),
            jax.ShapeDtypeStruct((SEQ, D), BF),
            jax.ShapeDtypeStruct((D, SEQ), BF),
        ],
        scratch_shapes=[pltpu.VMEM((D, D), BF), pltpu.SemaphoreType.DMA((len(layout),))],
        compiler_params=params(),
        cost_estimate=cost(6 * RATE, 16 * SEQ * D),
        name="hidden_units",
    )(a0, a1, x, gains, *blocks, *deps)


def feed_kernel(lead, width, size, base, order_in, order_out, *refs):
    gathered = order_in is None
    n2, n2t, cot, cott = refs[:4]
    blocks, refs = refs[4 : 6 if gathered else 12], refs[6 if gathered else 12 :]
    if not lead:
        bo_in, ng_in = refs[:2]
        refs = refs[2:]
    keep, send, bo_out, ng_out = refs[:4]
    n2_v, n2t_v, cot_v, cott_v, w, stage, bo, ng, mix_v, gu_v, sem_w, sem_o, sem_i = refs[4:]
    half, q = D // 2, D // 8
    tiles = width // FT

    def ordered_copies(lo, count):
        source, whole = blocks
        for j in range(3):

            def one(p, carry):
                a = pl.multiple_of(source[p] * size, size)
                col = j * width + lo * FT
                pltpu.make_async_copy(
                    whole.at[pl.ds(a, size), pl.ds(base + col, count * FT)],
                    w.at[pl.ds(pl.multiple_of(p * size, size), size), pl.ds(col, count * FT)],
                    sem_w.at[min(lo, 1), j],
                ).start()
                return carry

            lax.fori_loop(0, D // size, one, 0)

    def ordered_wait(lo, count):
        for j in range(3):
            cols = pl.ds(j * width + lo * FT, count * FT)
            pltpu.make_async_copy(
                blocks[1].at[:, pl.ds(base + j * width + lo * FT, count * FT)], w.at[:, cols], sem_w.at[min(lo, 1), j]
            ).wait()

    def weight_copies(f):
        out = []
        for j in range(3):
            col = pl.multiple_of(j * width + f * FT, FT)
            for r, src in enumerate(blocks):
                out.append(
                    pltpu.make_async_copy(
                        src.at[:, pl.ds(col, FT)], w.at[pl.ds(r * q, q), pl.ds(col, FT)], sem_w.at[f, 8 * j + r]
                    )
                )
        return out

    def term_copies(g):
        col = pl.multiple_of(g * FT, FT)
        return [
            pltpu.make_async_copy(
                stage.at[pl.ds(s * half + p * q, q), pl.ds(col, FT)],
                dst.at[pl.ds(r * q, q), pl.ds(col, FT)],
                sem_o.at[g, 4 * s + r],
            )
            for s, dst in enumerate((keep, send))
            for r, p in enumerate(order_out)
        ]

    first = [pltpu.make_async_copy(n2, n2_v, sem_i.at[0]), pltpu.make_async_copy(cot, cot_v, sem_i.at[1])]
    second = [pltpu.make_async_copy(n2t, n2t_v, sem_i.at[2]), pltpu.make_async_copy(cott, cott_v, sem_i.at[3])]
    sums_in = []
    if not lead:
        sums_in = [pltpu.make_async_copy(bo_in, bo, sem_i.at[4]), pltpu.make_async_copy(ng_in, ng, sem_i.at[5])]
    sums_out = [pltpu.make_async_copy(bo, bo_out, sem_i.at[6]), pltpu.make_async_copy(ng, ng_out, sem_i.at[7])]
    if gathered:
        ordered_copies(0, 1)
        for c in first:
            c.start()
        ordered_copies(1, tiles - 1)
    else:
        for c in weight_copies(0) + first:
            c.start()
        for f in range(1, tiles):
            for c in weight_copies(f):
                c.start()
    for c in sums_in + second:
        c.start()
    for c in first:
        c.wait()

    def units(f, carry):
        if gathered:
            pl.when(f == 0)(lambda: ordered_wait(0, 1))
            pl.when(f == 1)(lambda: ordered_wait(1, tiles - 1))
        else:
            for c in weight_copies(f):
                c.wait()
        at = [pl.ds(pl.multiple_of(j * width + f * FT, FT), FT) for j in range(3)]

        def tokens(i, inner):
            rows = pl.ds(pl.multiple_of(i * TILE, TILE), TILE)
            n = n2_v[rows, :]
            gate = nn(n, w[:, at[0]])
            upward = nn(n, w[:, at[1]])
            mixed_grad = nn(cot_v[rows, :], w[:, at[2]])
            square = gate * gate
            bend = jnp.tanh(gate * (GELU_A + (GELU_A * GELU_B) * square))
            curve = 0.5 * (1.0 + bend)
            active = gate * curve
            slope = curve + (0.5 * gate) * (1.0 - bend * bend) * (GELU_A + (3.0 * GELU_A * GELU_B) * square)
            mix_v[rows, at[0]] = (active * upward).astype(BF)
            gu_v[rows, at[0]] = (mixed_grad * upward * slope).astype(BF)
            gu_v[rows, at[1]] = (mixed_grad * active).astype(BF)
            return inner

        lax.fori_loop(0, SEQ // TILE, tokens, 0)
        return carry

    lax.fori_loop(0, tiles, units, 0)
    for c in sums_in:
        c.wait()

    def sums(i, carry):
        rows = pl.ds(pl.multiple_of(i * TILE, TILE), TILE)
        for j in range(2):
            cols = slice(j * TILE, (j + 1) * TILE)
            one = nt(mix_v[rows, :], w[cols, 2 * width :])
            two = nt(gu_v[rows, :], w[cols, : 2 * width])
            bo[rows, cols] = one if lead else bo[rows, cols] + one
            ng[rows, cols] = two if lead else ng[rows, cols] + two
        return carry

    lax.fori_loop(0, SEQ // TILE, sums, 0)
    for c in sums_out:
        c.start()
    for c in second:
        c.wait()

    def terms(left, right, start):
        def one(f, carry):
            cols = pl.ds(pl.multiple_of(f * FT, FT), FT)
            out = pl.ds(pl.multiple_of(start * FT + f * FT, FT), FT)
            stage[:, out] = nn(left[...], right[:, cols]).astype(BF)
            for c in term_copies(start + f):
                c.start()
            return carry

        return one

    lax.fori_loop(0, 2 * tiles, terms(n2t_v, gu_v, 0), 0)
    lax.fori_loop(0, tiles, terms(cott_v, mix_v, 2 * tiles), 0)
    for c in sums_out:
        c.wait()

    def drain(g, carry):
        for c in term_copies(g):
            c.wait()
        return carry

    lax.fori_loop(0, 3 * tiles, drain, 0)


def feed(n2, n2t, cot, cott, blocks, width, sums, size, base, order_in, order_out, deps=()):
    lead = sums is None
    tiles = width // FT
    acts = [n2, n2t, cot, cott, *blocks] + ([] if lead else list(sums))
    half = jax.ShapeDtypeStruct((D // 2, 3 * width), BF)
    total = jax.ShapeDtypeStruct((SEQ, D), F32)
    bf = lambda *s: pltpu.VMEM(s, BF)
    return pl.pallas_call(
        after(functools.partial(feed_kernel, lead, width, size, base, order_in, order_out), len(acts), deps),
        in_specs=[ANY] * 4 + [ANY if order_in else SMEM] + [ANY] * (len(acts) - 5 + len(deps)),
        out_specs=[ANY] * 4,
        out_shape=[half, half, total, total],
        scratch_shapes=[
            bf(SEQ, D), bf(D, SEQ), bf(SEQ, D), bf(D, SEQ), bf(D, 3 * width), bf(D, 3 * width),
            pltpu.VMEM((SEQ, D), F32), pltpu.VMEM((SEQ, D), F32),
            bf(SEQ, width), bf(SEQ, 2 * width),
            pltpu.SemaphoreType.DMA((tiles, 24)), pltpu.SemaphoreType.DMA((3 * tiles, 8)), pltpu.SemaphoreType.DMA((8,)),
        ],
        compiler_params=pltpu.CompilerParams(vmem_limit_bytes=VLIM),
        cost_estimate=cost(27 * RATE, 12 * D * width + 24 * SEQ * D, SEQ * width),
        name="feed_forward",
    )(*acts, *deps)


def middle_kernel(layout, count, *refs):
    h_ref, ng_ref, c_ref, gains_ref = refs[:4]
    blocks = refs[4 : 4 + count]
    hg_ref, bt_ref, ag_ref, gain_ref, w, sems = refs[4 + count :]

    @pl.when(pl.program_id(0) == 0)
    def _():
        fetch(blocks, layout, w, sems)
        gain_ref[...] = jnp.zeros_like(gain_ref)

    hidden = h_ref[...]
    grad = ng_ref[...]
    scale = scaled_rows(hidden)
    gain_ref[0:1, :] += jnp.sum(grad * hidden * scale, axis=0, keepdims=True)
    grad = grad * gains_ref[1:2, :]
    mean = jnp.mean(grad * hidden, axis=-1, keepdims=True)
    out = c_ref[...].astype(F32) + (scale * grad - hidden * (scale * scale * scale * mean))
    hg_ref[...] = out
    low = out.astype(BF)
    bt_ref[...] = low.T
    ag_ref[...] = nn(low, w[...]).astype(BF)


def middle(hidden, ng, cot, gains, blocks, layout, deps=()):
    rows = TILE
    tok = lambda c: pl.BlockSpec((rows, c), lambda i: (i, 0))
    n = len(blocks)
    return pl.pallas_call(
        after(functools.partial(middle_kernel, layout, n), 4 + n, deps),
        grid=(SEQ // rows,),
        in_specs=[tok(D), tok(D), tok(D), pl.BlockSpec((8, D), lambda i: (0, 0))] + [ANY] * (n + len(deps)),
        out_specs=[tok(D), pl.BlockSpec((D, rows), lambda i: (0, i)), tok(D), pl.BlockSpec((8, D), lambda i: (0, 0))],
        out_shape=[
            jax.ShapeDtypeStruct((SEQ, D), F32),
            jax.ShapeDtypeStruct((D, SEQ), BF),
            jax.ShapeDtypeStruct((SEQ, D), BF),
            jax.ShapeDtypeStruct((8, D), F32),
        ],
        scratch_shapes=[pltpu.VMEM((D, D), BF), pltpu.SemaphoreType.DMA((len(layout),))],
        compiler_params=params(),
        cost_estimate=cost(7 * RATE, 20 * SEQ * D),
        name="hidden_gradient",
    )(hidden, ng, cot, gains, *blocks, *deps)


def terms_kernel(lefts, order, *refs):
    count = sum(n for n in lefts)
    left_refs, rights = refs[: len(lefts)], refs[len(lefts) : len(lefts) + count]
    keep, send = refs[len(lefts) + count :]
    q = D // 8

    def work(out):
        at, r = 0, 0
        for left, n in zip(left_refs, lefts):
            for right in rights[r : r + n]:
                wide = right.shape[1]
                part = nn(left[...], right[...]).astype(BF)
                for j, p in enumerate(order):
                    out[j * q : (j + 1) * q, at : at + wide] = part[p * q : (p + 1) * q]
                at += wide
            r += n

    @pl.when(pl.program_id(0) == 0)
    def _():
        work(keep)

    @pl.when(pl.program_id(0) == 1)
    def _():
        work(send)


def weight_terms(sets, order, deps=()):
    lefts = [s[0] for s in sets]
    rights = [r for s in sets for r in s[1]]
    counts = tuple(len(s[1]) for s in sets)
    width = sum(r.shape[1] for r in rights)
    half = D // 2
    sh = jax.ShapeDtypeStruct((half, width), BF)
    n = len(lefts) + len(rights)
    out = pl.BlockSpec((half, width), lambda i: (0, 0))
    return pl.pallas_call(
        after(functools.partial(terms_kernel, counts, order), n, deps),
        grid=(2,),
        in_specs=[pl.BlockSpec((half, SEQ), lambda i: (i, 0)) for _ in lefts]
        + [pl.BlockSpec(r.shape, lambda i: (0, 0)) for r in rights]
        + [ANY] * len(deps),
        out_specs=[out, out],
        out_shape=[sh, sh],
        compiler_params=params(),
        cost_estimate=cost(4 * RATE * width / 1536, 4 * SEQ * D + 4 * D * width),
        name="weight_terms",
    )(*lefts, *rights, *deps)


def last_kernel(size, layout, count, blocks_n, *refs):
    back_ref, x_ref, hg_ref, gains_ref = refs[:4]
    grads = refs[4 : 4 + count]
    blocks = refs[4 + count : 4 + count + blocks_n]
    out_ref, gain_ref, w, scratch, sems = refs[4 + count + blocks_n :]

    @pl.when(pl.program_id(0) == 0)
    def _():
        fetch(blocks, layout, w, sems)
        gain_ref[...] = jnp.zeros_like(gain_ref)

    grad = nt(jnp.concatenate([g[...] for g in grads], axis=1), w[...])
    x = x_ref[...].astype(F32)
    scale = scaled_rows(x)
    gain_ref[0:1, :] += jnp.sum(grad * x * scale, axis=0, keepdims=True)
    grad = grad * gains_ref[0:1, :]
    mean = jnp.mean(grad * x, axis=-1, keepdims=True)
    scratch[...] = hg_ref[...] + (scale * grad - x * (scale * scale * scale * mean))
    for q, chunk in shift_blocks(lambda at: scratch[:, pl.ds(at, BLK)], back_ref, size):
        out_ref[:, q * BLK : (q + 1) * BLK] = chunk


def last(back, x, hg, gains, grads, blocks, layout, size, deps=()):
    rows = TILE
    tok = lambda c: pl.BlockSpec((rows, c), lambda i: (i, 0))
    n = 4 + len(grads) + len(blocks)
    return pl.pallas_call(
        after(functools.partial(last_kernel, size, layout, len(grads), len(blocks)), n, deps),
        grid=(SEQ // rows,),
        in_specs=[SMEM, tok(D), tok(D), pl.BlockSpec((8, D), lambda i: (0, 0))]
        + [tok(g.shape[1]) for g in grads]
        + [ANY] * (len(blocks) + len(deps)),
        out_specs=[tok(D), pl.BlockSpec((8, D), lambda i: (0, 0))],
        out_shape=[jax.ShapeDtypeStruct((SEQ, D), F32), jax.ShapeDtypeStruct((8, D), F32)],
        scratch_shapes=[
            pltpu.VMEM((D, 6 * GROUP), BF), pltpu.VMEM((rows, D), F32), pltpu.SemaphoreType.DMA((len(layout),)),
        ],
        compiler_params=params(),
        cost_estimate=cost(14 * RATE, 20 * SEQ * D),
        name="input_gradient",
    )(back, x, hg, gains, *grads, *blocks, *deps)


def output_kernel(size, back_ref, seg_ref, h_ref, bo_ref, out_ref, scratch):
    live = seg_ref[...] > 0
    scratch[...] = h_ref[...] + bo_ref[...]
    for q, chunk in shift_blocks(lambda at: scratch[:, pl.ds(at, BLK)], back_ref, size):
        out_ref[:, q * BLK : (q + 1) * BLK] = jnp.where(live, chunk, 0.0).astype(BF)


def block_output_of(back, segk, hidden, bo, size, deps=()):
    rows = 256
    tok = lambda c: pl.BlockSpec((rows, c), lambda i: (i, 0))
    return pl.pallas_call(
        after(functools.partial(output_kernel, size), 4, deps),
        grid=(SEQ // rows,),
        in_specs=[SMEM, tok(BLK), tok(D), tok(D)] + [ANY] * len(deps),
        out_specs=tok(D),
        out_shape=jax.ShapeDtypeStruct((SEQ, D), BF),
        scratch_shapes=[pltpu.VMEM((rows, D), F32)],
        compiler_params=params(),
        cost_estimate=cost(7 * RATE, 10 * SEQ * D),
        name="block_output",
    )(back, segk, hidden, bo, *deps)


def gains_kernel(size, back_ref, one_ref, two_ref, out_ref):
    for j, ref in enumerate((one_ref, two_ref)):
        for q, chunk in shift_blocks(lambda at: ref[:, pl.ds(at, BLK)], back_ref, size):
            out_ref[8 * j + q : 8 * j + q + 1, :] = chunk[0:1]


def natural_gains(back, one, two, size, deps=()):
    return pl.pallas_call(
        after(functools.partial(gains_kernel, size), 3, deps),
        in_specs=[SMEM, pl.BlockSpec(memory_space=pltpu.VMEM), pl.BlockSpec(memory_space=pltpu.VMEM)] + [ANY] * len(deps),
        out_specs=pl.BlockSpec(memory_space=pltpu.VMEM),
        out_shape=jax.ShapeDtypeStruct((16, BLK), F32),
        name="gain_terms",
    )(back, one, two, *deps)


NATURAL = (0, 1, 2, 3)
CROSSED = (0, 2, 1, 3)


class Slice:
    def __init__(self, mesh):
        self.count = mesh.shape["dp"] * mesh.shape["fsdp"]
        self.inner = mesh.shape["fsdp"]
        self.core = self.inner
        bits = [1 << b for b in range(self.count.bit_length() - 1)]
        self.rest = [b for b in reversed(bits) if b not in (1, 2, self.core)]
        self.order = [self.core, 2, 1] + self.rest[::-1]
        self.size = D // self.count

    def place(self, index):
        p = index * 0
        for b in self.order:
            p = 2 * p + (index // b) % 2
        return p

    def swap(self, x, bit):
        return lax.ppermute(x, AXES, [(i, i ^ bit) for i in range(self.count)])

    def sum_all(self, x):
        for bit in self.rest + [1, 2, self.core]:
            x = x + self.swap(x, bit)
        return x


class Order:
    def __init__(self):
        self.token = None

    def hold(self, args):
        leaves, tree = jax.tree.flatten(args)
        at = [i for i, x in enumerate(leaves) if hasattr(x, "aval")]
        if self.token is not None:
            held = lax.optimization_barrier([leaves[i] for i in at] + [self.token])
            for i, x in zip(at, held):
                leaves[i] = x
        return jax.tree.unflatten(tree, leaves)

    def __call__(self, f, *args):
        out = f(*self.hold(args))
        self.token = jax.tree.leaves(out)[0]
        return out


class Chain:
    def __init__(self, links, run):
        self.links, self.run, self.pending = links, run, []


def meet(run, *chains):
    arrays = run.hold([c.pending for c in chains] + [run.token])
    run.token = arrays.pop()
    for c, got in zip(chains, arrays):
        c.met(got)
        c.pending = []


class Gather(Chain):
    def __init__(self, links, run, shard, bit):
        super().__init__(links, run)
        self.line, self.bit, self.bits = run.hold(shard), bit, list(links.rest)
        self.pending = [links.swap(self.line, self.bits.pop(0))]

    def met(self, got):
        self.got = got

    def step(self):
        swap = self.links.swap
        self.line = self.run(join, self.line, self.got[0])
        if self.bits:
            self.pending = [swap(self.line, self.bits.pop(0))]
        else:
            self.pending = [swap(self.line, 1), swap(self.line, 2)]

    def corner(self):
        swap, core = self.links.swap, self.links.core
        across, along = self.got
        self.blocks = [self.line, across, along]
        self.others = [swap(b, core) for b in self.blocks]
        self.pending = [swap(across, 2) if self.bit == 2 else swap(along, 1)]

    def end(self):
        self.blocks.append(self.got[0])
        self.others.append(self.links.swap(self.got[0], self.links.core))
        return tuple(self.blocks + self.others)


class Scatter(Chain):
    def __init__(self, links, run, keep, send):
        super().__init__(links, run)
        self.terms, self.rows, self.bits = [keep], D // 8, links.rest[::-1]
        self.pending = [links.swap(run.hold(send), links.core)]

    def met(self, got):
        self.got = got

    def corner(self):
        self.terms += self.got
        send = self.run(add_terms, [(t, 3 * self.rows) for t in self.terms], self.rows)
        self.pending = [self.links.swap(send, 2)]

    def sides(self):
        along = self.run(add_terms, [(t, 2 * self.rows) for t in self.terms], self.rows)
        along = self.links.swap(along, 2)
        across = self.run(add_terms, [(t, self.rows) for t in self.terms] + [(self.got[0], 0)], self.rows)
        self.pending = [along, self.links.swap(across, 1)]

    def step(self):
        self.terms += self.got
        half = self.rows // 2
        send = self.run(add_terms, [(t, half) for t in self.terms], half)
        self.rows = half
        self.pending = [self.links.swap(send, self.bits.pop(0))]

    def ends(self):
        if self.pending:
            meet(self.run, self)
        while self.bits:
            self.step()
            meet(self.run, self)
        return self.terms + self.got


def on_device(
    links,
    layer_input,
    segment_ids,
    relative_buckets,
    first_gain,
    query_weight,
    key_weight,
    value_weight,
    output_projection,
    relative_table,
    second_gain,
    gate_weight,
    up_weight,
    down_projection,
    output_cotangent,
):
    size = links.size
    me = lax.axis_index("dp") * links.inner + lax.axis_index("fsdp")
    place = np.array([links.place(i) for i in range(links.count)], np.int32)
    index = np.argsort(place).astype(np.int32)
    source = jnp.asarray(index) ^ me
    back = jnp.asarray(place) ^ links.place(me)

    gains_shard = jnp.pad(jnp.stack([first_gain, second_gain], axis=1), ((0, 0), (0, BLK - 2)))
    w1, w2, w3 = PIECES
    feed_shards = (gate_weight, up_weight, down_projection)
    qkv_shards = (query_weight, key_weight, value_weight)
    triple = lambda lo, hi: tuple((n, lo, hi) for n in range(3))
    run = Order()
    segk = jnp.broadcast_to(segment_ids[:, None], (SEQ, BLK))
    segq = jnp.where(segment_ids > 0, segment_ids, -1).reshape(NB, BLK)
    spans = ranges(segment_ids)
    one_hot = (relative_buckets[::-1][:, None] == jnp.arange(BUCKETS)[None, :]).astype(BF)
    one_hot = jnp.pad(one_hot, ((0, 1), (0, 0)))
    offsets = lax.dot_general(relative_table, one_hot, (((0,), (1,)), ((), ())), preferred_element_type=F32)

    (first_shard,) = run(pack, qkv_shards + (gains_shard,), (triple(0, GROUP) + ((3, 0, BLK),),))
    first = Gather(links, run, first_shard, 2)
    (x,) = run(prepare, source, layer_input, segk, size, False)
    meet(run, first)
    first.step()
    (second_shard,) = run(pack, qkv_shards + (output_projection,), (triple(GROUP, 2 * GROUP) + ((3, 0, D),),))
    second = Gather(links, run, second_shard, 1)
    cot, cott = run(prepare, source, output_cotangent, segk, size, True)
    meet(run, first)
    first.step()
    while len(first.pending) < 2:
        meet(run, first)
        first.step()
    f1_shard, late_shard = run(
        pack,
        feed_shards,
        (triple(0, w1), tuple((n, lo, lo + w) for lo, w in ((w1, w2), (w1 + w2, w3)) for n in range(3))),
    )
    late = lax.all_gather(late_shard, AXES, axis=0, tiled=True)
    meet(run, second)
    second.step()
    strips = run(make_strips, offsets.reshape(HEADS // 2, 2, 2 * SEQ))
    meet(run, first)
    first.corner()
    while len(second.pending) < 2:
        meet(run, second)
        second.step()
    f1 = Gather(links, run, f1_shard, 2)
    meet(run, first)
    lead_blocks = first.end()
    layout0 = layout_of(lead_blocks, NATURAL, 3 * GROUP + BLK)
    qkv0, normed, turned, gains = run(project, x, lead_blocks, layout0, True)
    meet(run, second, f1)
    second.corner()
    f1.step()
    att0, lse0 = run(attn_fwd, spans, segk, segq, strips, qkv0, 0)
    meet(run, second, f1)
    next_blocks = second.end()
    f1.step()
    while len(f1.pending) < 2:
        meet(run, f1)
        f1.step()
    layout1 = layout_of(next_blocks, NATURAL, 3 * GROUP)
    layout_o = layout_of(next_blocks, NATURAL, D, 3 * GROUP)
    (qkv1,) = run(project, normed, next_blocks, layout1, False)
    meet(run, f1)
    f1.corner()
    att1, lse1 = run(attn_fwd, spans, segk, segq, strips, qkv1, 4)
    meet(run, f1)
    f1_blocks = f1.end()
    hidden, n2, n2t = run(hidden_units, att0, att1, x, gains, next_blocks, layout_o)
    acts = (n2, n2t, cot, cott)
    keep, send, bo, ng = run(feed, *acts, f1_blocks, w1, None, size, 0, NATURAL, NATURAL)
    s1 = Scatter(links, run, keep, send)
    meet(run, s1)
    s1.corner()
    keep, send, bo, ng = run(feed, *acts, (source, late), w2, (bo, ng), size, 0, None, NATURAL)
    meet(run, s1)
    s2 = Scatter(links, run, keep, send)
    s1.sides()
    meet(run, s2)
    s2.corner()
    keep, send, bo, ng = run(feed, *acts, (source, late), w3, (bo, ng), size, 3 * w2, None, NATURAL)
    meet(run, s1, s2)
    s3 = Scatter(links, run, keep, send)
    s2.sides()
    s1.step()
    meet(run, s3)
    s3.corner()
    hidden_grad, branch_t, attended_grad, second_term = run(middle, hidden, ng, cot, gains, next_blocks, layout_o)
    meet(run, s1)
    s1.step()

    def back_pairs(qkv, lse, first_pair):
        return run(attn_bwd, spans, segk, segq, strips, qkv, attended_grad, lse, first_pair)

    side = lambda a, b: [z for j in range(3) for z in (a[j], b[j])]
    g0 = back_pairs(qkv0, lse0, 0)
    meet(run, s1, s2)
    s2.step()
    g1 = back_pairs(qkv0, lse0, 2)
    meet(run, s2, s3)
    s3.sides()
    s2.step()
    keep, send = run(weight_terms, [(branch_t, [att0, att1]), (turned, side(g0, g1))], NATURAL)
    meet(run, s2)
    s4 = Scatter(links, run, keep, send)
    meet(run, s4)
    s4.corner()
    g2 = back_pairs(qkv1, lse1, 4)
    meet(run, s3)
    s3.step()
    g3 = back_pairs(qkv1, lse1, 6)
    meet(run, s3, s4)
    s4.sides()
    s3.step()
    keep, send = run(weight_terms, [(turned, side(g2, g3))], NATURAL)
    meet(run, s3)
    s5 = Scatter(links, run, keep, send)
    meet(run, s5)
    s5.corner()
    block_output = run(block_output_of, back, segk, hidden, bo, size)
    meet(run, s4, s5)
    s5.sides()
    s4.step()
    input_gradient, first_term = run(
        last, back, x, hidden_grad, gains, side(g0, g1) + side(g2, g3), lead_blocks + next_blocks,
        layout_of(lead_blocks, NATURAL, 3 * GROUP)
        + tuple((n + len(lead_blocks), *l) for n, *l in layout_of(next_blocks, NATURAL, 3 * GROUP, 0, 3 * GROUP)),
        size,
    )
    meet(run, s4, s5)
    s5.step()
    s4.step()
    gain_rows = run(natural_gains, back, first_term, second_term, size)
    offset_grads = jnp.concatenate([g[3] for g in (g0, g1, g2, g3)], axis=0).reshape(HEADS, 2 * SEQ)
    table_term = lax.dot_general(
        one_hot.astype(F32), offset_grads, (((0,), (1,)), ((), ())), precision=HIGHEST, preferred_element_type=F32
    )
    small = jnp.concatenate(
        [gain_rows, table_term.reshape(-1, BLK), jnp.zeros((4, BLK), F32)], axis=0
    )
    small = links.sum_all(small)
    gain_sums = small[:16].reshape(2, D)
    mine = lax.dynamic_slice_in_dim(gain_sums, me * size, size, 1)
    table_gradient = small[16:20].reshape(BUCKETS, HEADS)
    grads = finish([s.ends() for s in (s4, s5, s1, s2, s3)], size)
    return (block_output, input_gradient, *grads, mine[0], mine[1], table_gradient)


def solution(mesh):
    rows, flat, full = P(AXES, None), P(AXES), P()
    return jax.shard_map(
        functools.partial(on_device, Slice(mesh)),
        mesh=mesh,
        in_specs=(rows, flat, full, flat, rows, rows, rows, rows, full, flat, rows, rows, rows, rows),
        out_specs=(rows,) * 9 + (flat, flat, full),
        check_vma=False,
    )
```

time: 697 us -> 534 us (0.77)
  waiting for transfers between devices: 185 us -> 91.6 us
  starting transfers between devices: 104 us -> 70.8 us
  Pallas kernels: 301 us -> 277 us
  local copies, waits for them, and re-layouts: 37.6 us -> 15.2 us
  between operations: 2.21 us -> 15 us
    ppermute x90 -> x62, waiting for transfers between devices: 185 us -> 91.6 us  [swap(): return lax.ppermute(x, AXES, [(i, i ^ bit) for i in range(self.count)])]
    convert_element_type x6 -> x22, other arithmetic: 2.44 us -> 46.8 us  [add_terms(): return sum((t[off:off + rows].astype(F32) for t, off in terms)).astype(BF)]
    ppermute x90 -> x62, starting transfers between devices: 104 us -> 70.8 us  [swap(): return lax.ppermute(x, AXES, [(i, i ^ bit) for i in range(self.count)])]
    pallas_call x19 -> x25, Pallas kernels: 301 us -> 277 us  [the longest x3 85.8 us: feed(): pl.pallas_call(after(functools.partial(feed_kernel, lead, width, size, ba...]
    concatenate x38 -> x2, other arithmetic: 25.8 us -> 2.29 us  [the longest x1 1.52 us: on_device(): jnp.concatenate([g[3] for g in (g0, g1, g2, g3)], axis=0)]
    slice x34 -> x0, local copies, waits for them, and re-layouts: 11.5 us -> none  [the longest x5 3.41 us: on_device(): parts = [gate_weight[:, cols], up_weight[:, cols], down_projection[:, cols]]]
    unnamed x143 -> x93, local copies, waits for them, and re-layouts: 19.8 us -> 8.59 us
    another operation x12 -> x0, other arithmetic: 8.48 us -> none
  transfers between devices with their start and end apart: 90 -> 63, of which waited for: 35 -> 23; matrix products, arithmetic and copies ran while one was open for 12% -> 9% of each run, Pallas kernels for 28% -> 51%
where the time goes in v2:
time: 534 us; the launch traced here: 527 us
  Pallas kernels  277 us (52%)
  waiting for transfers between devices  91.6 us (17%)
  starting transfers between devices  70.8 us (13%)
  other arithmetic  54.2 us (10%)
  local copies, waits for them, and re-layouts  15.2 us (3%)
  between operations  15 us (3%)
    ppermute x62, waiting for transfers between devices, swap(): return lax.ppermute(x, AXES, [(i, i ^ bit) for i in range(self.count)])  91.6 us
    pallas_call x3, Pallas kernels, feed(): pl.pallas_call(after(functools.partial(feed_kernel, lead, width, size, ba...  85.8 us
    ppermute x62, starting transfers between devices, swap(): return lax.ppermute(x, AXES, [(i, i ^ bit) for i in range(self.count)])  70.8 us
    pallas_call x4, Pallas kernels, attn_bwd(): pl.pallas_call(after(functools.partial(attn_bwd_kernel, unit), 9, deps),...  48.3 us
    convert_element_type x22, other arithmetic, add_terms(): return sum((t[off:off + rows].astype(F32) for t, off in terms)).astype(BF)  46.8 us
    pallas_call x2, Pallas kernels, attn_fwd(): pl.pallas_call(after(functools.partial(attn_fwd_kernel, unit), 7, deps),...  23.7 us
    pallas_call x1, Pallas kernels, last(): pl.pallas_call(after(functools.partial(last_kernel, size, layout, len(gra...  21.3 us
    pallas_call x2, Pallas kernels, weight_terms(): pl.pallas_call(after(functools.partial(terms_kernel, counts, order), n, d...  18.9 us
  transfers between devices with their start and end apart: 63, of which 23 were waited for; matrix products, arithmetic and copies ran while one was open for 9% of the time, Pallas kernels for 51%

profile of v2, /device:TPU:0, one launch (start us, length us, event | category | flops | bytes accessed | tf_op | source)
XLA Modules:
  0.0 526.6 jit_solution(6713673989093424306)
XLA Ops:
  26.2 7.3 %prepare.3 = (bf16[1024,1024]{1,0:T(8,128)(2,1)}, bf16[1024,1024]{1,0:T(8,128)(2,1)}) custom-call(s32[32]{0:T(128)} %broadcast_xor_fusion.src_ref.refs_4_, bf16[1024,1024]{1,0:T(8,128)(2,1)} %x_ref.1, s32[1024,128]{1,0:T(8,128)} %broadcast_in_dim.11.seg_ref.segk_ref), custom_call_target="tpu_custom_call" | custom-call | flops 5000000000 | bytes 5242880 | tf_op jit(solution)/shard_map/prepare/pallas_call | solution.py:326
  47.7 9.8 %bias_strips.1.strip = f32[8,1920,256]{2,1,0:T(8,128)} custom-call(f32[8,2,2048]{2,1,0:T(2,128)} %reshape.59.rev_ref), custom_call_target="tpu_custom_call" | custom-call | tf_op jit(solution)/shard_map/bias_strips/pallas_call | solution.py:89
  64.6 14.5 %collective-permute-done.5.refs_4_.refs_19_ = bf16[128,1664]{1,0:T(8,128)(2,1)S(1)} collective-permute-done((bf16[128,1664]{1,0:T(8,128)(2,1)S(1)}, bf16[128,1664]{1,0:T(8,128)(2,1)S(1)}, u32[]{:S(2)}, u32[]{:S(2)}) %collective-permute-start.5) | collective-permute-done | bytes 426016 | tf_op jit(solution)/shard_map/ppermute | solution.py:901
  85.2 10.3 %query_key_value.2 = (bf16[1024,1536]{1,0:T(8,128)(2,1)}, bf16[1024,1024]{1,0:T(8,128)(2,1)}, bf16[1024,1024]{1,0:T(8,128)(2,1)}, f32[8,1024]{1,0:T(8,128)}) custom-call(bf16[1024,1024]{1,0:T(8,128)(2,1)} %prepare.2.refs_0_.refs_2_.refs_1_, bf16[128,1664]{1,0:T(8,128)(2,1)} %copy-done.25, bf16[128,1664]{1,0:T(8,128)(2,1)} %copy-done.37, ...), custom_call_target="tpu_custom_call" | custom-call | flops 6000000000 | bytes 7602176 | tf_op jit(solution)/shard_map/query_key_value/pallas_call | solution.py:477
  99.3 11.6 %attention_forward.2 = (bf16[1024,512]{1,0:T(8,128)(2,1)}, f32[4,8,256]{2,1,0:T(8,128)}) custom-call(s32[16]{0:T(128)} %pad_add_fusion.rng_ref, s32[1024,128]{1,0:T(8,128)} %broadcast_in_dim.11.seg_ref.segk_ref, s32[8,128]{1,0:T(8,128)} %fusion.2.segq_ref, f32[8,1920,256]{2,1,0:T(8,128)} %bias_strips.1.strip, ...), custom_call_target="tpu_custom_call" | custom-call | flops 12999999488 | bytes 4194304 | tf_op jit(solution)/shard_map/attention_forward/pallas_call | solution.py:218
  110.9 11.7 %collective-permute-done.15 = bf16[64,2304]{1,0:T(8,128)(2,1)S(1)} collective-permute-done((bf16[64,2304]{1,0:T(8,128)(2,1)S(1)}, bf16[64,2304]{1,0:T(8,128)(2,1)S(1)}, u32[]{:S(2)}, u32[]{:S(2)}) %collective-permute-start.15) | collective-permute-done | bytes 294944 | tf_op jit(solution)/shard_map/ppermute | solution.py:901
  122.6 5.8 %collective-permute-done.14.refs_4_.refs_7_.refs_27_ = bf16[128,2560]{1,0:T(8,128)(2,1)} collective-permute-done((bf16[128,2560]{1,0:T(8,128)(2,1)S(1)}, bf16[128,2560]{1,0:T(8,128)(2,1)}, u32[]{:S(2)}, u32[]{:S(2)}) %collective-permute-start.14) | collective-permute-done | bytes 655392 | tf_op jit(solution)/shard_map/ppermute | solution.py:901
  131.1 8.5 %query_key_value.3.q_ref.k_ref.v_ref = bf16[1024,1536]{1,0:T(8,128)(2,1)} custom-call(bf16[1024,1024]{1,0:T(8,128)(2,1)} %get-tuple-element.450.refs_0_, bf16[128,2560]{1,0:T(8,128)(2,1)} %copy-done.22, bf16[128,2560]{1,0:T(8,128)(2,1)} %copy-done.29, bf16[128,2560]{1,0:T(8,128)(2,1)} %copy-done.30, ...), custom_call_target="tpu_custom_call" | custom-call | flops 6000000000 | bytes 7340032 | tf_op jit(solution)/shard_map/query_key_value/pallas_call | solution.py:477
  139.6 9.6 %collective-permute-done.20.refs_5_ = bf16[128,2304]{1,0:T(8,128)(2,1)S(1)} collective-permute-done((bf16[128,2304]{1,0:T(8,128)(2,1)S(1)}, bf16[128,2304]{1,0:T(8,128)(2,1)S(1)}, u32[]{:S(2)}, u32[]{:S(2)}) %collective-permute-start.20) | collective-permute-done | bytes 589856 | tf_op jit(solution)/shard_map/ppermute | solution.py:901
  151.5 12.0 %attention_forward.3 = (bf16[1024,512]{1,0:T(8,128)(2,1)}, f32[4,8,256]{2,1,0:T(8,128)}) custom-call(s32[16]{0:T(128)} %pad_add_fusion.rng_ref, s32[1024,128]{1,0:T(8,128)} %broadcast_in_dim.11.seg_ref.segk_ref, s32[8,128]{1,0:T(8,128)} %fusion.2.segq_ref, f32[8,1920,256]{2,1,0:T(8,128)} %bias_strips.1.strip, ...), custom_call_target="tpu_custom_call" | custom-call | flops 12999999488 | bytes 4194304 | tf_op jit(solution)/shard_map/attention_forward/pallas_call | solution.py:218
  166.7 8.8 %hidden_units.1 = (f32[1024,1024]{1,0:T(8,128)}, bf16[1024,1024]{1,0:T(8,128)(2,1)}, bf16[1024,1024]{1,0:T(8,128)(2,1)}) custom-call(bf16[1024,512]{1,0:T(8,128)(2,1)} %get-tuple-element.620.refs_0_.refs_2_, bf16[1024,512]{1,0:T(8,128)(2,1)} %get-tuple-element.621.refs_1_.refs_3_, bf16[1024,1024]{1,0:T(8,128)(2,1)} %prepare.2.refs_0_.refs_2_.refs_1_, ...), custom_call_target="tpu_custom_call" | custom-call | flops 6000000000 | bytes 16777216 | tf_op jit(solution)/shard_map/hidden_units/pallas_call | solution.py:510
  176.6 24.3 %feed_forward.3 = (bf16[512,2304]{1,0:T(8,128)(2,1)}, bf16[512,2304]{1,0:T(8,128)(2,1)}, f32[1024,1024]{1,0:T(8,128)}, f32[1024,1024]{1,0:T(8,128)}) custom-call(bf16[1024,1024]{1,0:T(8,128)(2,1)} %get-tuple-element.529.refs_0_, bf16[1024,1024]{1,0:T(8,128)(2,1)} %get-tuple-element.530.refs_1_, bf16[1024,1024]{1,0:T(8,128)(2,1)} %get-tuple-element.561.refs_2_, ...), custom_call_target="tpu_custom_call" | custom-call | flops 27000000512 | bytes 34603008 | tf_op jit(solution)/shard_map/feed_forward/pallas_call | solution.py:687
  208.9 30.7 %feed_forward.4 = (bf16[512,3072]{1,0:T(8,128)(2,1)}, bf16[512,3072]{1,0:T(8,128)(2,1)}, f32[1024,1024]{1,0:T(8,128)}, f32[1024,1024]{1,0:T(8,128)}) custom-call(bf16[1024,1024]{1,0:T(8,128)(2,1)} %get-tuple-element.529.refs_0_, bf16[1024,1024]{1,0:T(8,128)(2,1)} %get-tuple-element.530.refs_1_, bf16[1024,1024]{1,0:T(8,128)(2,1)} %get-tuple-element.561.refs_2_, ...), custom_call_target="tpu_custom_call" | custom-call | flops 27000000512 | bytes 37748736 | tf_op jit(solution)/shard_map/feed_forward/pallas_call | solution.py:687
  249.9 30.9 %feed_forward.5 = (bf16[512,3072]{1,0:T(8,128)(2,1)}, bf16[512,3072]{1,0:T(8,128)(2,1)}, f32[1024,1024]{1,0:T(8,128)}, f32[1024,1024]{1,0:T(8,128)}) custom-call(bf16[1024,1024]{1,0:T(8,128)(2,1)} %get-tuple-element.529.refs_0_, bf16[1024,1024]{1,0:T(8,128)(2,1)} %get-tuple-element.530.refs_1_, bf16[1024,1024]{1,0:T(8,128)(2,1)} %get-tuple-element.561.refs_2_, ...), custom_call_target="tpu_custom_call" | custom-call | flops 27000000512 | bytes 37748736 | tf_op jit(solution)/shard_map/feed_forward/pallas_call | solution.py:687
  295.0 10.6 %hidden_gradient.1 = (f32[1024,1024]{1,0:T(8,128)}, bf16[1024,1024]{1,0:T(8,128)(2,1)}, bf16[1024,1024]{1,0:T(8,128)(2,1)}, f32[8,1024]{1,0:T(8,128)}) custom-call(f32[1024,1024]{1,0:T(8,128)} %get-tuple-element.687.refs_0_.h_ref, f32[1024,1024]{1,0:T(8,128)} %get-tuple-element.560.refs_1_, bf16[1024,1024]{1,0:T(8,128)(2,1)} %get-tuple-element.561.refs_2_, ...), custom_call_target="tpu_custom_call" | custom-call | flops 7000000000 | bytes 20971520 | tf_op jit(solution)/shard_map/hidden_gradient/pallas_call | solution.py:731
  308.3 12.2 %attention_backward.4 = (bf16[1024,256]{1,0:T(8,128)(2,1)}, bf16[1024,256]{1,0:T(8,128)(2,1)}, bf16[1024,256]{1,0:T(8,128)(2,1)}, f32[2,2,2048]{2,1,0:T(2,128)}) custom-call(s32[16]{0:T(128)} %pad_add_fusion.rng_ref, s32[1024,128]{1,0:T(8,128)} %broadcast_in_dim.11.seg_ref.segk_ref, s32[8,128]{1,0:T(8,128)} %fusion.2.segq_ref, ...), custom_call_target="tpu_custom_call" | custom-call | flops 12000000000 | bytes 4194304 | tf_op jit(solution)/shard_map/attention_backward/pallas_call | solution.py:250
  326.4 12.0 %attention_backward.5 = (bf16[1024,256]{1,0:T(8,128)(2,1)}, bf16[1024,256]{1,0:T(8,128)(2,1)}, bf16[1024,256]{1,0:T(8,128)(2,1)}, f32[2,2,2048]{2,1,0:T(2,128)}) custom-call(s32[16]{0:T(128)} %pad_add_fusion.rng_ref, s32[1024,128]{1,0:T(8,128)} %broadcast_in_dim.11.seg_ref.segk_ref, s32[8,128]{1,0:T(8,128)} %fusion.2.segq_ref, ...), custom_call_target="tpu_custom_call" | custom-call | flops 12000000000 | bytes 4194304 | tf_op jit(solution)/shard_map/attention_backward/pallas_call | solution.py:250
  347.9 11.3 %weight_terms.2 = (bf16[512,2560]{1,0:T(8,128)(2,1)}, bf16[512,2560]{1,0:T(8,128)(2,1)}) custom-call(bf16[1024,1024]{1,0:T(8,128)(2,1)} %get-tuple-element.618.refs_0_, bf16[1024,1024]{1,0:T(8,128)(2,1)} %get-tuple-element.671.refs_1_.refs_0_, bf16[1024,512]{1,0:T(8,128)(2,1)} %get-tuple-element.620.refs_0_.refs_2_, ...), custom_call_target="tpu_custom_call" | custom-call | flops 6666666496 | bytes 14680064 | tf_op jit(solution)/shard_map/weight_terms/pallas_call | solution.py:784
  368.0 12.2 %attention_backward.6 = (bf16[1024,256]{1,0:T(8,128)(2,1)}, bf16[1024,256]{1,0:T(8,128)(2,1)}, bf16[1024,256]{1,0:T(8,128)(2,1)}, f32[2,2,2048]{2,1,0:T(2,128)}) custom-call(s32[16]{0:T(128)} %pad_add_fusion.rng_ref, s32[1024,128]{1,0:T(8,128)} %broadcast_in_dim.11.seg_ref.segk_ref, s32[8,128]{1,0:T(8,128)} %fusion.2.segq_ref, ...), custom_call_target="tpu_custom_call" | custom-call | flops 12000000000 | bytes 4194304 | tf_op jit(solution)/shard_map/attention_backward/pallas_call | solution.py:250
  388.5 12.0 %attention_backward.7 = (bf16[1024,256]{1,0:T(8,128)(2,1)}, bf16[1024,256]{1,0:T(8,128)(2,1)}, bf16[1024,256]{1,0:T(8,128)(2,1)}, f32[2,2,2048]{2,1,0:T(2,128)}) custom-call(s32[16]{0:T(128)} %pad_add_fusion.rng_ref, s32[1024,128]{1,0:T(8,128)} %broadcast_in_dim.11.seg_ref.segk_ref, s32[8,128]{1,0:T(8,128)} %fusion.2.segq_ref, ...), custom_call_target="tpu_custom_call" | custom-call | flops 12000000000 | bytes 4194304 | tf_op jit(solution)/shard_map/attention_backward/pallas_call | solution.py:250
  409.1 7.7 %weight_terms.3 = (bf16[512,1536]{1,0:T(8,128)(2,1)}, bf16[512,1536]{1,0:T(8,128)(2,1)}) custom-call(bf16[1024,1024]{1,0:T(8,128)(2,1)} %get-tuple-element.671.refs_1_.refs_0_, bf16[1024,256]{1,0:T(8,128)(2,1)} %get-tuple-element.709.refs_1_.refs_10_, bf16[1024,256]{1,0:T(8,128)(2,1)} %get-tuple-element.710.refs_2_.refs_11_, ...), custom_call_target="tpu_custom_call" | custom-call | flops 4000000000 | bytes 10485760 | tf_op jit(solution)/shard_map/weight_terms/pallas_call | solution.py:784
  437.8 7.4 %block_output.1 = bf16[1024,1024]{1,0:T(8,128)(2,1)} custom-call(s32[32]{0:T(128)} %broadcast_xor_fusion.1.back_ref.refs_0_, s32[1024,128]{1,0:T(8,128)} %broadcast_in_dim.11.seg_ref.segk_ref, f32[1024,1024]{1,0:T(8,128)} %get-tuple-element.687.refs_0_.h_ref, f32[1024,1024]{1,0:T(8,128)} %get-tuple-element.688.bo_ref), custom_call_target="tpu_custom_call" | custom-call | flops 7000000000 | bytes 10485760 | tf_op jit(solution)/shard_map/block_output/pallas_call | solution.py:851
  455.6 21.3 %input_gradient.1 = (f32[1024,1024]{1,0:T(8,128)}, f32[8,1024]{1,0:T(8,128)}) custom-call(s32[32]{0:T(128)} %broadcast_xor_fusion.1.back_ref.refs_0_, bf16[1024,1024]{1,0:T(8,128)(2,1)} %prepare.2.refs_0_.refs_2_.refs_1_, f32[1024,1024]{1,0:T(8,128)} %get-tuple-element.701.refs_2_, f32[8,1024]{1,0:T(8,128)} %get-tuple-element.702.refs_3_, ...), custom_call_target="tpu_custom_call" | custom-call | flops 14000000000 | bytes 20971520 | tf_op jit(solution)/shard_map/input_gradient/pallas_call | solution.py:824
  505.8 7.4 %collective-permute-done.54.refs_5_ = bf16[32,2560]{1,0:T(8,128)(2,1)S(1)} collective-permute-done((bf16[32,2560]{1,0:T(8,128)(2,1)}, bf16[32,2560]{1,0:T(8,128)(2,1)S(1)}, u32[]{:S(2)}, u32[]{:S(2)}) %collective-permute-start.54) | collective-permute-done | bytes 163872 | tf_op jit(solution)/shard_map/ppermute | solution.py:901
  (283 shorter events, 201.9 us)
Async XLA Ops:
  7.2 201.7 %all-gather.2.cloned.1.call-start = ((), (), s32[]{:S(2)}) async-start(), calls=%async_computation | async-start | bytes 12976128 | tf_op jit(solution)/shard_map/all_gather | solution.py:1062
  38.5 23.8 %collective-permute-start.3 = (bf16[128,1664]{1,0:T(8,128)(2,1)S(1)}, bf16[128,1664]{1,0:T(8,128)(2,1)S(1)}, u32[]{:S(2)}, u32[]{:S(2)}) collective-permute-start(bf16[128,1664]{1,0:T(8,128)(2,1)S(1)} %constant_dynamic-update-slice_fusion.2.refs_1_.refs_16_), channel_id=1, source_target_pairs={{0,1},{1,0},{2,3},{3,2},{4,5},{5,4},{6,7},{7,6},{8,9},{9,8},{10,11... | collective-permute-start | bytes 1277960 | tf_op jit(solution)/shard_map/ppermute | solution.py:901
  40.1 22.3 %collective-permute-start.4 = (bf16[128,1664]{1,0:T(8,128)(2,1)S(1)}, bf16[128,1664]{1,0:T(8,128)(2,1)}, u32[]{:S(2)}, u32[]{:S(2)}) collective-permute-start(bf16[128,1664]{1,0:T(8,128)(2,1)S(1)} %constant_dynamic-update-slice_fusion.2.refs_1_.refs_16_), channel_id=1, source_target_pairs={{0,2},{1,3},{2,0},{3,1},{4,6},{5,7},{6,4},{7,5},{8,10},{9,11},{10,... | collective-permute-start | bytes 1277960 | tf_op jit(solution)/shard_map/ppermute | solution.py:901
  47.7 33.6 %collective-permute-start.7 = (bf16[128,1664]{1,0:T(8,128)(2,1)S(1)}, bf16[128,1664]{1,0:T(8,128)(2,1)}, u32[]{:S(2)}, u32[]{:S(2)}) collective-permute-start(bf16[128,1664]{1,0:T(8,128)(2,1)S(1)} %constant_dynamic-update-slice_fusion.2.refs_1_.refs_16_), channel_id=1, source_target_pairs={{0,4},{1,5},{2,6},{3,7},{4,0},{5,1},{6,2},{7,3},{8,12},{9,13},{10,... | collective-permute-start | bytes 1277960 | tf_op jit(solution)/shard_map/ppermute | solution.py:901
  83.6 45.8 %collective-permute-start.16 = (bf16[128,2560]{1,0:T(8,128)(2,1)S(1)}, bf16[128,2560]{1,0:T(8,128)(2,1)S(1)}, u32[]{:S(2)}, u32[]{:S(2)}) collective-permute-start(bf16[128,2560]{1,0:T(8,128)(2,1)S(1)} %constant_dynamic-update-slice_fusion.6.refs_1_.refs_4_.refs_24_), channel_id=1, source_target_pairs={{0,4},{1,5},{2,6},{3,7},{4,0},{5,1},{6,2},{7,3},{8,12},{9,13},{10,... | collective-permute-start | bytes 1966088 | tf_op jit(solution)/shard_map/ppermute | solution.py:901
  98.1 30.3 %collective-permute-start.14 = (bf16[128,2560]{1,0:T(8,128)(2,1)S(1)}, bf16[128,2560]{1,0:T(8,128)(2,1)}, u32[]{:S(2)}, u32[]{:S(2)}) collective-permute-start(bf16[128,2560]{1,0:T(8,128)(2,1)S(1)} %collective-permute-done.12.refs_3_.refs_6_.refs_26_), channel_id=1, source_target_pairs={{0,1},{1,0},{2,3},{3,2},{4,5},{5,4},{6,7},{7,6},{8,9},{9,8},{10,11... | collective-permute-start | bytes 1966088 | tf_op jit(solution)/shard_map/ppermute | solution.py:901
  98.6 32.5 %collective-permute-start.18 = (bf16[128,2560]{1,0:T(8,128)(2,1)S(1)}, bf16[128,2560]{1,0:T(8,128)(2,1)}, u32[]{:S(2)}, u32[]{:S(2)}) collective-permute-start(bf16[128,2560]{1,0:T(8,128)(2,1)S(1)} %collective-permute-done.12.refs_3_.refs_6_.refs_26_), channel_id=1, source_target_pairs={{0,4},{1,5},{2,6},{3,7},{4,0},{5,1},{6,2},{7,3},{8,12},{9,13},{10,... | collective-permute-start | bytes 1966088 | tf_op jit(solution)/shard_map/ppermute | solution.py:901
  98.6 24.0 %collective-permute-start.15 = (bf16[64,2304]{1,0:T(8,128)(2,1)S(1)}, bf16[64,2304]{1,0:T(8,128)(2,1)S(1)}, u32[]{:S(2)}, u32[]{:S(2)}) collective-permute-start(bf16[64,2304]{1,0:T(8,128)(2,1)S(1)} %constant_dynamic-update-slice_fusion.8), channel_id=1, source_target_pairs={{0,8},{1,9},{2,10},{3,11},{4,12},{5,13},{6,14},{7,15},{8,0},{9,1},... | collective-permute-start | bytes 884744 | tf_op jit(solution)/shard_map/ppermute | solution.py:901
  98.7 32.3 %collective-permute-start.17 = (bf16[128,2560]{1,0:T(8,128)(2,1)S(1)}, bf16[128,2560]{1,0:T(8,128)(2,1)}, u32[]{:S(2)}, u32[]{:S(2)}) collective-permute-start(bf16[128,2560]{1,0:T(8,128)(2,1)S(1)} %collective-permute-done.11.refs_2_.refs_5_.refs_25_), channel_id=1, source_target_pairs={{0,4},{1,5},{2,6},{3,7},{4,0},{5,1},{6,2},{7,3},{8,12},{9,13},{10,... | collective-permute-start | bytes 1966088 | tf_op jit(solution)/shard_map/ppermute | solution.py:901
  131.0 44.5 %collective-permute-start.23 = (bf16[128,2304]{1,0:T(8,128)(2,1)S(1)}, bf16[128,2304]{1,0:T(8,128)(2,1)S(1)}, u32[]{:S(2)}, u32[]{:S(2)}) collective-permute-start(bf16[128,2304]{1,0:T(8,128)(2,1)S(1)} %constant_dynamic-update-slice_fusion.10.refs_4_), channel_id=1, source_target_pairs={{0,4},{1,5},{2,6},{3,7},{4,0},{5,1},{6,2},{7,3},{8,12},{9,13},{10,... | collective-permute-start | bytes 1769480 | tf_op jit(solution)/shard_map/ppermute | solution.py:901
  151.0 24.5 %collective-permute-start.24 = (bf16[128,2304]{1,0:T(8,128)(2,1)S(1)}, bf16[128,2304]{1,0:T(8,128)(2,1)S(1)}, u32[]{:S(2)}, u32[]{:S(2)}) collective-permute-start(bf16[128,2304]{1,0:T(8,128)(2,1)S(1)} %collective-permute-done.20.refs_5_), channel_id=1, source_target_pairs={{0,4},{1,5},{2,6},{3,7},{4,0},{5,1},{6,2},{7,3},{8,12},{9,13},{10,... | collective-permute-start | bytes 1769480 | tf_op jit(solution)/shard_map/ppermute | solution.py:901
  151.0 24.5 %collective-permute-start.25 = (bf16[128,2304]{1,0:T(8,128)(2,1)S(1)}, bf16[128,2304]{1,0:T(8,128)(2,1)}, u32[]{:S(2)}, u32[]{:S(2)}) collective-permute-start(bf16[128,2304]{1,0:T(8,128)(2,1)S(1)} %collective-permute-done.21.refs_6_), channel_id=1, source_target_pairs={{0,4},{1,5},{2,6},{3,7},{4,0},{5,1},{6,2},{7,3},{8,12},{9,13},{10,... | collective-permute-start | bytes 1769480 | tf_op jit(solution)/shard_map/ppermute | solution.py:901
  208.3 31.3 %collective-permute-start.28 = (bf16[128,2304]{1,0:T(8,128)(2,1)S(1)}, bf16[128,2304]{1,0:T(8,128)(2,1)}, u32[]{:S(2)}, u32[]{:S(2)}) collective-permute-start(bf16[128,2304]{1,0:T(8,128)(2,1)S(1)} %add_convert_fusion.11), channel_id=1, source_target_pairs={{0,2},{1,3},{2,0},{3,1},{4,6},{5,7},{6,4},{7,5},{8,10},{9,11},{10,... | collective-permute-start | bytes 1769480 | tf_op jit(solution)/shard_map/ppermute | solution.py:901
  242.1 38.8 %collective-permute-start.30 = (bf16[128,2304]{1,0:T(8,128)(2,1)}, bf16[128,2304]{1,0:T(8,128)(2,1)S(1)}, u32[]{:S(2)}, u32[]{:S(2)}) collective-permute-start(bf16[128,2304]{1,0:T(8,128)(2,1)} %add_convert_fusion.10), channel_id=1, source_target_pairs={{0,2},{1,3},{2,0},{3,1},{4,6},{5,7},{6,4},{7,5},{8,10},{9,11},{10,... | collective-permute-start | bytes 1769480 | tf_op jit(solution)/shard_map/ppermute | solution.py:901
  246.0 34.8 %collective-permute-start.31 = (bf16[128,2304]{1,0:T(8,128)(2,1)}, bf16[128,2304]{1,0:T(8,128)(2,1)}, u32[]{:S(2)}, u32[]{:S(2)}) collective-permute-start(bf16[128,2304]{1,0:T(8,128)(2,1)} %add_convert_fusion.9), channel_id=1, source_target_pairs={{0,1},{1,0},{2,3},{3,2},{4,5},{5,4},{6,7},{7,6},{8,9},{9,8},{10,11... | collective-permute-start | bytes 1769480 | tf_op jit(solution)/shard_map/ppermute | solution.py:901
  249.4 31.5 %collective-permute-start.32 = (bf16[128,3072]{1,0:T(8,128)(2,1)}, bf16[128,3072]{1,0:T(8,128)(2,1)}, u32[]{:S(2)}, u32[]{:S(2)}) collective-permute-start(bf16[128,3072]{1,0:T(8,128)(2,1)} %add_convert_fusion.5), channel_id=1, source_target_pairs={{0,2},{1,3},{2,0},{3,1},{4,6},{5,7},{6,4},{7,5},{8,10},{9,11},{10,... | collective-permute-start | bytes 2359304 | tf_op jit(solution)/shard_map/ppermute | solution.py:901
  284.1 36.4 %collective-permute-start.36 = (bf16[128,3072]{1,0:T(8,128)(2,1)}, bf16[128,3072]{1,0:T(8,128)(2,1)S(1)}, u32[]{:S(2)}, u32[]{:S(2)}) collective-permute-start(bf16[128,3072]{1,0:T(8,128)(2,1)} %add_convert_fusion.4), channel_id=1, source_target_pairs={{0,2},{1,3},{2,0},{3,1},{4,6},{5,7},{6,4},{7,5},{8,10},{9,11},{10,... | collective-permute-start | bytes 2359304 | tf_op jit(solution)/shard_map/ppermute | solution.py:901
  288.3 32.2 %collective-permute-start.37 = (bf16[128,3072]{1,0:T(8,128)(2,1)}, bf16[128,3072]{1,0:T(8,128)(2,1)}, u32[]{:S(2)}, u32[]{:S(2)}) collective-permute-start(bf16[128,3072]{1,0:T(8,128)(2,1)} %add_convert_fusion.3), channel_id=1, source_target_pairs={{0,1},{1,0},{2,3},{3,2},{4,5},{5,4},{6,7},{7,6},{8,9},{9,8},{10,11... | collective-permute-start | bytes 2359304 | tf_op jit(solution)/shard_map/ppermute | solution.py:901
  294.7 43.7 %collective-permute-start.39 = (bf16[128,3072]{1,0:T(8,128)(2,1)}, bf16[128,3072]{1,0:T(8,128)(2,1)}, u32[]{:S(2)}, u32[]{:S(2)}) collective-permute-start(bf16[128,3072]{1,0:T(8,128)(2,1)} %get-tuple-element.833), channel_id=1, source_target_pairs={{0,2},{1,3},{2,0},{3,1},{4,6},{5,7},{6,4},{7,5},{8,10},{9,11},{10,... | collective-permute-start | bytes 2359304 | tf_op jit(solution)/shard_map/ppermute | solution.py:901
  359.2 21.3 %collective-permute-start.42 = (bf16[128,3072]{1,0:T(8,128)(2,1)}, bf16[128,3072]{1,0:T(8,128)(2,1)S(1)}, u32[]{:S(2)}, u32[]{:S(2)}) collective-permute-start(bf16[128,3072]{1,0:T(8,128)(2,1)} %get-tuple-element.832), channel_id=1, source_target_pairs={{0,2},{1,3},{2,0},{3,1},{4,6},{5,7},{6,4},{7,5},{8,10},{9,11},{10,... | collective-permute-start | bytes 2359304 | tf_op jit(solution)/shard_map/ppermute | solution.py:901
  421.9 23.2 %collective-permute-start.48 = (bf16[128,2560]{1,0:T(8,128)(2,1)}, bf16[128,2560]{1,0:T(8,128)(2,1)S(1)}, u32[]{:S(2)}, u32[]{:S(2)}) collective-permute-start(bf16[128,2560]{1,0:T(8,128)(2,1)} %get-tuple-element.834), channel_id=1, source_target_pairs={{0,2},{1,3},{2,0},{3,1},{4,6},{5,7},{6,4},{7,5},{8,10},{9,11},{10,... | collective-permute-start | bytes 1966088 | tf_op jit(solution)/shard_map/ppermute | solution.py:901
  435.8 41.2 %collective-permute-start.52 = (bf16[128,1536]{1,0:T(8,128)(2,1)}, bf16[128,1536]{1,0:T(8,128)(2,1)S(1)}, u32[]{:S(2)}, u32[]{:S(2)}) collective-permute-start(bf16[128,1536]{1,0:T(8,128)(2,1)} %get-tuple-element.836), channel_id=1, source_target_pairs={{0,2},{1,3},{2,0},{3,1},{4,6},{5,7},{6,4},{7,5},{8,10},{9,11},{10,... | collective-permute-start | bytes 1179656 | tf_op jit(solution)/shard_map/ppermute | solution.py:901
  450.5 26.5 %collective-permute-start.53 = (bf16[128,1536]{1,0:T(8,128)(2,1)}, bf16[128,1536]{1,0:T(8,128)(2,1)}, u32[]{:S(2)}, u32[]{:S(2)}) collective-permute-start(bf16[128,1536]{1,0:T(8,128)(2,1)} %add_convert_fusion.12), channel_id=1, source_target_pairs={{0,1},{1,0},{2,3},{3,2},{4,5},{5,4},{6,7},{7,6},{8,9},{9,8},{10,11... | collective-permute-start | bytes 1179656 | tf_op jit(solution)/shard_map/ppermute | solution.py:901
  455.6 21.3 %collective-permute-start.51 = (bf16[64,2560]{1,0:T(8,128)(2,1)}, bf16[64,2560]{1,0:T(8,128)(2,1)}, u32[]{:S(2)}, u32[]{:S(2)}) collective-permute-start(bf16[64,2560]{1,0:T(8,128)(2,1)} %add_convert_fusion.17), channel_id=1, source_target_pairs={{0,8},{1,9},{2,10},{3,11},{4,12},{5,13},{6,14},{7,15},{8,0},{9,1},... | collective-permute-start | bytes 983048 | tf_op jit(solution)/shard_map/ppermute | solution.py:901
  (81 other events, 1045.0 us)
Sparse Core Ops, SparseCore 0:
  35.8 122.7 all-gather.1
